TPU v7x, 32 devices: a whole 2x2x4 slice. The times are simulated.
32 devices in a mesh: band: 8 (over z, y), batch: 4 (over x, core).
Axes of the slice: x: 2, y: 2, z: 4, core: 2. Of those that a mesh axis runs over, the one named last changes fastest.
Arguments:
- activations: bfloat16 [64, 1, 1024, 384], P('band', None, 'batch'), may hold values from -6 to 6
- cotangent: bfloat16 [64, 1, 1024, 384], P('band', None, 'batch'), may hold values from -6 to 6
- frame_counts: int32 [1], replicated, may hold values from 896 to 1024, as said below
- slot_bands: int32 [64], replicated, may hold values from -1 to 61, as said below
- time_prenorm: bfloat16 [384], replicated, may hold values from 0.5 to 1.5
- time_project: bfloat16 [384, 1536], replicated, may hold values from -0.3125 to 0.3125
- time_gating: bfloat16 [384, 8], replicated, may hold values from -0.3125 to 0.3125
- time_output: bfloat16 [512, 384], replicated, may hold values from -6 to 6
- time_midnorm: bfloat16 [384], replicated, may hold values from 0.5 to 1.5
- time_expand: bfloat16 [384, 1536], replicated, may hold values from -0.3125 to 0.3125
- time_shrink: bfloat16 [1536, 384], replicated, may hold values from -0.15625 to 0.15625
- band_prenorm: bfloat16 [384], replicated, may hold values from 0.5 to 1.5
- band_project: bfloat16 [384, 1536], replicated, may hold values from -0.3125 to 0.3125
- band_gating: bfloat16 [384, 8], replicated, may hold values from -0.3125 to 0.3125
- band_output: bfloat16 [512, 384], replicated, may hold values from -3 to 3
- band_midnorm: bfloat16 [384], replicated, may hold values from 0.5 to 1.5
- band_expand: bfloat16 [384, 1536], replicated, may hold values from -0.3125 to 0.3125
- band_shrink: bfloat16 [1536, 384], replicated, may hold values from -0.15625 to 0.15625
Outputs:
- layer_output: bfloat16 [64, 1, 1024, 384], P('band', None, 'batch')
- input_grad: float32 [64, 1, 1024, 384], P('band', None, 'batch')
- time_prenorm_grad: float32 [384], replicated
- time_project_grad: float32 [384, 1536], replicated
- time_gating_grad: float32 [384, 8], replicated
- time_output_grad: float32 [512, 384], replicated
- time_midnorm_grad: float32 [384], replicated
- time_expand_grad: float32 [384, 1536], replicated
- time_shrink_grad: float32 [1536, 384], replicated
- band_prenorm_grad: float32 [384], replicated
- band_project_grad: float32 [384, 1536], replicated
- band_gating_grad: float32 [384, 8], replicated
- band_output_grad: float32 [512, 384], replicated
- band_midnorm_grad: float32 [384], replicated
- band_expand_grad: float32 [384, 1536], replicated
- band_shrink_grad: float32 [1536, 384], replicated
Inputs may be any that keep to these rules, and one draw needn't show every extreme that they name: `frame_counts`: real frames come first. `slot_bands`: each band 0 to 61 stands in exactly one slot; the other 2 slots hold -1.
All inputs are finite; a program needn't handle non-finite values.
Results may differ from a plain program's by a relative error of at most 0.03.
Values may be sent and summed in bfloat16 or wider, within the bound.
A program may use at most 448 MiB of HBM per device.

v0:
```python
import math

import jax
import jax.numpy as jnp
from jax import lax
from jax.experimental import pallas as pl
from jax.experimental.pallas import tpu as pltpu
from jax.sharding import PartitionSpec as P

EPSILON = 1e-05
NEG_FILL = -1000000000.0
TIME_LAYOUT = ("bqhe", "bkhe")
BAND_LAYOUT = ("qbhe", "kbhe")


def rms_scale(residual, gain):
    return (
        residual * lax.rsqrt(jnp.mean(residual * residual, axis=-1, keepdims=True) + EPSILON) * gain
    )


def gelu_exact(values):
    return jax.nn.gelu(values, approximate=False)


def rotary_tables(positions, head_size):
    half_size = head_size // 2
    rates = jnp.exp(-math.log(10000.0) * jnp.arange(half_size, dtype=jnp.float32) / half_size)
    angles = positions[:, None] * rates[None, :]
    return (jnp.cos(angles), jnp.sin(angles))


def rotate(vectors, cos_table, sin_table):
    half_size = vectors.shape[-1] // 2
    first = vectors[..., :half_size]
    second = vectors[..., half_size:]
    return jnp.concatenate(
        [first * cos_table - second * sin_table, first * sin_table + second * cos_table], axis=-1
    )


def token_sum(left, right):
    return lax.dot_general(
        left.reshape(-1, left.shape[-1]),
        right.reshape(-1, right.shape[-1]),
        (((0,), (0,)), ((), ())),
        preferred_element_type=jnp.float32,
    )


def back_dot(gradient, weight):
    return lax.dot_general(
        gradient,
        weight,
        (((gradient.ndim - 1,), (1,)), ((), ())),
        preferred_element_type=jnp.float32,
    )


def block_forward(queries, key_rows, value_rows, key_valid, layout):
    query_form, key_form = layout
    scores = (
        jnp.einsum(
            query_form + "," + key_form + "->bhqk",
            queries,
            key_rows,
            preferred_element_type=jnp.float32,
        )
        * 0.125
    )
    scores = jnp.where(key_valid[:, None, None, :], scores, NEG_FILL)
    highest = jnp.max(scores, axis=-1, keepdims=True)
    exponents = jnp.exp(scores - highest)
    totals = jnp.sum(exponents, axis=-1, keepdims=True)
    soft_weights = (exponents / totals).astype(jnp.bfloat16)
    output = jnp.einsum(
        "bhqk," + key_form + "->" + query_form,
        soft_weights,
        value_rows,
        preferred_element_type=jnp.float32,
    )
    return (output, highest + jnp.log(totals))


def block_backward(queries, key_rows, value_rows, key_valid, log_totals, out_grad, layout):
    query_form, key_form = layout
    scores = (
        jnp.einsum(
            query_form + "," + key_form + "->bhqk",
            queries,
            key_rows,
            preferred_element_type=jnp.float32,
        )
        * 0.125
    )
    soft_weights = jnp.where(key_valid[:, None, None, :], jnp.exp(scores - log_totals), 0.0)
    weight_grad = jnp.einsum(
        query_form + "," + key_form + "->bhqk",
        out_grad,
        value_rows,
        preferred_element_type=jnp.float32,
    )
    score_grad = (
        soft_weights * (weight_grad - jnp.sum(soft_weights * weight_grad, axis=-1, keepdims=True))
    ).astype(jnp.bfloat16)
    query_grad = (
        jnp.einsum(
            "bhqk," + key_form + "->" + query_form,
            score_grad,
            key_rows,
            preferred_element_type=jnp.float32,
        )
        * 0.125
    )
    key_grad = (
        jnp.einsum(
            "bhqk," + query_form + "->" + key_form,
            score_grad,
            queries,
            preferred_element_type=jnp.float32,
        )
        * 0.125
    )
    value_grad = jnp.einsum(
        "bhqk," + query_form + "->" + key_form,
        soft_weights.astype(jnp.bfloat16),
        out_grad,
        preferred_element_type=jnp.float32,
    )
    return (query_grad, key_grad, value_grad)


def time_attend(queries, key_rows, value_rows, key_valid):
    keys_full, values_full = (
        lax.all_gather(key_rows, "batch", axis=1, tiled=True),
        lax.all_gather(value_rows, "batch", axis=1, tiled=True),
    )
    output, log_totals = block_forward(queries, keys_full, values_full, key_valid, TIME_LAYOUT)
    return (output, (log_totals, keys_full, values_full))


def time_attend_back(queries, key_rows, value_rows, key_valid, attn_kept, out_grad):
    log_totals, keys_full, values_full = attn_kept
    query_grad, key_full_grad, value_full_grad = block_backward(
        queries, keys_full, values_full, key_valid, log_totals, out_grad, TIME_LAYOUT
    )
    key_grad, value_grad = (
        lax.psum_scatter(
            key_full_grad.astype(jnp.bfloat16), "batch", scatter_dimension=1, tiled=True
        ).astype(jnp.float32),
        lax.psum_scatter(
            value_full_grad.astype(jnp.bfloat16), "batch", scatter_dimension=1, tiled=True
        ).astype(jnp.float32),
    )
    return (query_grad, key_grad, value_grad)


def band_attend(queries, key_rows, value_rows, key_valid):
    return block_forward(queries, key_rows, value_rows, key_valid, BAND_LAYOUT)


def band_attend_back(queries, key_rows, value_rows, key_valid, attn_kept, out_grad):
    return block_backward(
        queries, key_rows, value_rows, key_valid, attn_kept, out_grad, BAND_LAYOUT
    )


def layer_forward(residual, params, tables, key_valid, attend):
    prenorm, project, gating, output_weight, midnorm, expand, shrink = params
    cos_table, sin_table = tables
    normed = rms_scale(residual, prenorm.astype(jnp.float32)).astype(jnp.bfloat16)
    projected = jnp.dot(normed, project, preferred_element_type=jnp.float32)
    gate_logits = jnp.dot(normed, gating, preferred_element_type=jnp.float32)
    inner_width = output_weight.shape[0]
    head_count = gating.shape[1]
    head_shape = residual.shape[:-1] + (head_count, inner_width // head_count)
    queries = rotate(projected[..., :inner_width].reshape(head_shape), cos_table, sin_table).astype(
        jnp.bfloat16
    )
    key_rows = rotate(
        projected[..., inner_width : 2 * inner_width].reshape(head_shape), cos_table, sin_table
    ).astype(jnp.bfloat16)
    value_rows = projected[..., 2 * inner_width :].reshape(head_shape).astype(jnp.bfloat16)
    attended, attn_kept = attend(queries, key_rows, value_rows, key_valid)
    gate_values = jax.nn.sigmoid(gate_logits)
    mixed_heads = (
        (attended * gate_values[..., None])
        .reshape(residual.shape[:-1] + (inner_width,))
        .astype(jnp.bfloat16)
    )
    middle = residual + jnp.dot(mixed_heads, output_weight, preferred_element_type=jnp.float32)
    normed_ffn = rms_scale(middle, midnorm.astype(jnp.float32)).astype(jnp.bfloat16)
    hidden = jnp.dot(normed_ffn, expand, preferred_element_type=jnp.float32)
    active = gelu_exact(hidden).astype(jnp.bfloat16)
    result = middle + jnp.dot(active, shrink, preferred_element_type=jnp.float32)
    kept_values = (
        residual,
        normed,
        gate_logits,
        queries,
        key_rows,
        value_rows,
        attn_kept,
        attended,
        mixed_heads,
        middle,
        normed_ffn,
        hidden,
        active,
    )
    return (result, kept_values)


def layer_backward(result_grad, params, kept_values, tables, key_valid, attend_back):
    prenorm, project, gating, output_weight, midnorm, expand, shrink = params
    (
        residual,
        normed,
        gate_logits,
        queries,
        key_rows,
        value_rows,
        attn_kept,
        attended,
        mixed_heads,
        middle,
        normed_ffn,
        hidden,
        active,
    ) = kept_values
    cos_table, sin_table = tables
    branch_grad = result_grad.astype(jnp.bfloat16)
    shrink_grad = token_sum(active, branch_grad)
    active_grad = back_dot(branch_grad, shrink)
    hidden_grad = jax.vjp(gelu_exact, hidden)[1](active_grad)[0].astype(jnp.bfloat16)
    expand_grad = token_sum(normed_ffn, hidden_grad)
    normed_ffn_grad = back_dot(hidden_grad, expand)
    middle_norm_grad, midnorm_grad = jax.vjp(rms_scale, middle, midnorm.astype(jnp.float32))[1](
        normed_ffn_grad
    )
    middle_grad = result_grad + middle_norm_grad
    attn_branch = middle_grad.astype(jnp.bfloat16)
    output_grad = token_sum(mixed_heads, attn_branch)
    mixed_grad = back_dot(attn_branch, output_weight).reshape(attended.shape)
    gate_values = jax.nn.sigmoid(gate_logits)
    attended_grad = (mixed_grad * gate_values[..., None]).astype(jnp.bfloat16)
    logit_grad = (
        jnp.sum(mixed_grad * attended, axis=-1) * gate_values * (1.0 - gate_values)
    ).astype(jnp.bfloat16)
    query_grad, key_grad, value_grad = attend_back(
        queries, key_rows, value_rows, key_valid, attn_kept, attended_grad
    )
    flat_shape = residual.shape[:-1] + (-1,)
    projected_grad = jnp.concatenate(
        [
            rotate(query_grad, cos_table, -sin_table).reshape(flat_shape),
            rotate(key_grad, cos_table, -sin_table).reshape(flat_shape),
            value_grad.reshape(flat_shape),
        ],
        axis=-1,
    ).astype(jnp.bfloat16)
    project_grad = token_sum(normed, projected_grad)
    gating_grad = token_sum(normed, logit_grad)
    normed_grad = back_dot(projected_grad, project) + back_dot(logit_grad, gating)
    residual_norm_grad, prenorm_grad = jax.vjp(rms_scale, residual, prenorm.astype(jnp.float32))[1](
        normed_grad
    )
    return (
        middle_grad + residual_norm_grad,
        (
            prenorm_grad,
            project_grad,
            gating_grad,
            output_grad,
            midnorm_grad,
            expand_grad,
            shrink_grad,
        ),
    )


def generic_shards(
    activations,
    cotangent,
    frame_counts,
    slot_bands,
    time_prenorm,
    time_project,
    time_gating,
    time_output,
    time_midnorm,
    time_expand,
    time_shrink,
    band_prenorm,
    band_project,
    band_gating,
    band_output,
    band_midnorm,
    band_expand,
    band_shrink,
):
    slot_dev, clip_count, frame_dev, model_width = activations.shape
    slot_count = slot_bands.shape[0]
    frames_all = frame_dev * lax.axis_size("batch")
    head_size = time_output.shape[0] // time_gating.shape[1]
    time_params = (
        time_prenorm,
        time_project,
        time_gating,
        time_output,
        time_midnorm,
        time_expand,
        time_shrink,
    )
    band_params = (
        band_prenorm,
        band_project,
        band_gating,
        band_output,
        band_midnorm,
        band_expand,
        band_shrink,
    )
    own_bands = lax.dynamic_slice_in_dim(slot_bands, lax.axis_index("band") * slot_dev, slot_dev)
    frame_start = lax.axis_index("batch") * frame_dev
    own_frames = frame_start + jnp.arange(frame_dev, dtype=jnp.int32)
    frame_valid = own_frames[None, :] < frame_counts[:, None]
    row_valid = (own_bands >= 0)[:, None, None] & frame_valid[None]
    full_valid = jnp.arange(frames_all, dtype=jnp.int32)[None, :] < frame_counts[:, None]
    time_valid = jnp.broadcast_to(full_valid[None], (slot_dev, clip_count, frames_all)).reshape(
        slot_dev * clip_count, frames_all
    )
    time_cos, time_sin = rotary_tables(own_frames.astype(jnp.float32), head_size)
    time_tables = (time_cos[None, :, None, :], time_sin[None, :, None, :])
    band_cos, band_sin = rotary_tables(jnp.maximum(slot_bands, 0).astype(jnp.float32), head_size)
    band_tables = (band_cos[:, None, None, :], band_sin[:, None, None, :])
    residual = activations.astype(jnp.float32).reshape(
        slot_dev * clip_count, frame_dev, model_width
    )
    time_result, time_kept = layer_forward(
        residual, time_params, time_tables, time_valid, time_attend
    )
    masked_cot = jnp.where(row_valid[..., None], cotangent, jnp.zeros((), jnp.bfloat16)).reshape(
        slot_dev, clip_count * frame_dev, model_width
    )
    frame_rows = lax.all_to_all(
        time_result.astype(jnp.bfloat16), "band", split_axis=1, concat_axis=0, tiled=True
    ).astype(time_result.dtype)
    band_valid = jnp.broadcast_to((slot_bands >= 0)[None, :], (frame_rows.shape[1], slot_count))
    band_result, band_kept = layer_forward(
        frame_rows, band_params, band_tables, band_valid, band_attend
    )
    back_rows = lax.all_to_all(
        band_result.astype(jnp.bfloat16), "band", split_axis=0, concat_axis=1, tiled=True
    ).astype(band_result.dtype)
    layer_output = jnp.where(
        row_valid[..., None], back_rows.reshape(activations.shape), 0.0
    ).astype(jnp.bfloat16)
    frame_cot = lax.all_to_all(masked_cot, "band", split_axis=1, concat_axis=0, tiled=True)
    frame_grad, band_grads = layer_backward(
        frame_cot.astype(jnp.float32),
        band_params,
        band_kept,
        band_tables,
        band_valid,
        band_attend_back,
    )
    slot_grad = lax.all_to_all(
        frame_grad.astype(jnp.bfloat16), "band", split_axis=0, concat_axis=1, tiled=True
    ).astype(frame_grad.dtype)
    input_grad, time_grads = layer_backward(
        slot_grad, time_params, time_kept, time_tables, time_valid, time_attend_back
    )
    input_grad = input_grad.reshape(activations.shape)
    all_grads = lax.psum(
        (
            time_grads[0],
            time_grads[1],
            time_grads[2],
            time_grads[3],
            time_grads[4],
            time_grads[5],
            time_grads[6],
            band_grads[0],
            band_grads[1],
            band_grads[2],
            band_grads[3],
            band_grads[4],
            band_grads[5],
            band_grads[6],
        ),
        ("band", "batch"),
    )
    return (
        layer_output,
        input_grad,
        all_grads[0],
        all_grads[1],
        all_grads[2],
        all_grads[3],
        all_grads[4],
        all_grads[5],
        all_grads[6],
        all_grads[7],
        all_grads[8],
        all_grads[9],
        all_grads[10],
        all_grads[11],
        all_grads[12],
        all_grads[13],
    )


BLOCK = 256
LOG2E = 1.4426950408889634
F32 = jnp.float32
BF16 = jnp.bfloat16
NN = (((1,), (0,)), ((), ()))
NT = (((1,), (1,)), ((), ()))
TN = (((0,), (0,)), ((), ()))
VMEM_BYTES = 60 * 2**20


def dg(left, right, dims):
    return lax.dot_general(left, right, dims, preferred_element_type=F32)


def norm_forward(rows, gain):
    scale = lax.rsqrt(jnp.mean(rows * rows, axis=0, keepdims=True) + EPSILON)
    return (rows * scale * gain).astype(BF16)


def norm_backward(rows, gain, grad):
    scale = lax.rsqrt(jnp.mean(rows * rows, axis=0, keepdims=True) + EPSILON)
    unit = rows * scale
    scaled = grad * gain
    inner = jnp.mean(scaled * unit, axis=0, keepdims=True)
    return scale * (scaled - unit * inner), grad * unit


def gelu_pair(values):
    size = jnp.abs(values)
    denominator = 1.0 + (0.3275911 * math.sqrt(0.5)) * size
    t = pl.reciprocal(denominator, approx=True)
    t = t * (2.0 - denominator * t)
    bell = jnp.exp2(values * values * (-0.5 * LOG2E))
    poly = 0.5 * 1.061405429
    for coefficient in (-1.453152027, 1.421413741, -0.284496736, 0.254829592):
        poly = poly * t + 0.5 * coefficient
    tail = poly * t * bell
    upper = jnp.where(values < 0.0, tail, 1.0 - tail)
    slope = upper + values * bell * (1.0 / math.sqrt(2.0 * math.pi))
    return values * upper, slope


def feed_forward(middle, normed, w1t_ref, w2t_ref, act_ref, slope_ref):
    part = w1t_ref.shape[0] // 3
    result = middle
    hidden = dg(w1t_ref[0:part, :], normed, NN)
    for i in range(3):
        rows = slice(i * part, (i + 1) * part)
        later = None
        if i < 2:
            later = dg(w1t_ref[(i + 1) * part : (i + 2) * part, :], normed, NN)
        active, slope = gelu_pair(hidden)
        active = active.astype(BF16)
        act_ref[rows, :] = active
        slope_ref[rows, :] = slope.astype(BF16)
        result = result + dg(w2t_ref[:, rows], active, NN)
        hidden = later
    return result


def turn(vectors, cos, sin):
    half = cos.shape[0]
    split = vectors.reshape(-1, 2 * half, vectors.shape[-1])
    first = split[:, :half]
    second = split[:, half:]
    turned = jnp.concatenate([first * cos - second * sin, first * sin + second * cos], axis=1)
    return turned.reshape(vectors.shape)


def three_parts(values):
    top = values.astype(BF16).astype(F32)
    rest = values - top
    middle = rest.astype(BF16).astype(F32)
    return top, middle, rest - middle


def extra_rows(rows, width):
    tile = jnp.concatenate(rows + [jnp.zeros((8 - len(rows), width), F32)], axis=0)
    return jnp.concatenate([tile, jnp.zeros((8, width), F32)], axis=0).astype(BF16)


def project_block(normed, wpt_ref, cos, sin, inner, scale):
    queries = turn(dg(wpt_ref[0:inner, :], normed, NN), cos, sin) * scale
    keys = turn(dg(wpt_ref[inner : 2 * inner, :], normed, NN), cos, sin)
    values = dg(wpt_ref[2 * inner : 3 * inner, :], normed, NN)
    return queries.astype(BF16), keys.astype(BF16), values.astype(BF16)


def column(gain_ref):
    row = gain_ref[...].astype(F32).reshape(1, gain_ref.shape[0])
    return jnp.broadcast_to(row, (8, row.shape[1])).T[:, :1]


def rotary_rows(positions, half):
    rank = lax.broadcasted_iota(jnp.int32, (half, positions.shape[1]), 0).astype(F32)
    angles = positions * jnp.exp(-math.log(10000.0) * rank / half)
    return jnp.cos(angles), jnp.sin(angles)


def flipped(ref):
    return ref[...].astype(F32).T.astype(BF16)


def greet_all(band_count, batch_count):
    count = band_count * batch_count
    me = lax.axis_index("band") * batch_count + lax.axis_index("batch")
    barrier = pltpu.get_barrier_semaphore()

    def signal(i, carry):
        other = lax.rem(me + i, count)
        pl.semaphore_signal(
            barrier,
            inc=1,
            device_id=(other // batch_count, lax.rem(other, batch_count)),
            device_id_type=pl.DeviceIdType.MESH,
        )
        return carry

    lax.fori_loop(1, count, signal, 0)
    pl.semaphore_wait(barrier, count - 1)


def send(source, target, send_sem, recv_sem, band, batch):
    pltpu.make_async_remote_copy(
        src_ref=source,
        dst_ref=target,
        send_sem=send_sem,
        recv_sem=recv_sem,
        device_id=(band, batch),
        device_id_type=pl.DeviceIdType.MESH,
    ).start()


def await_bytes(ref, sem):
    pltpu.make_async_copy(ref, ref, sem).wait()


class Place:
    def __init__(self):
        self.band, self.batch = lax.axis_index("band"), lax.axis_index("batch")
        self.bits = {
            "core": lax.rem(self.batch, 2),
            "x": self.batch // 2,
            "y": lax.rem(self.band, 2),
        }
        self.z = self.band // 2

    def across(self, axis):
        bit = self.bits[axis]
        if axis == "core":
            return self.band, self.batch + 1 - 2 * bit
        if axis == "x":
            return self.band, self.batch + 2 - 4 * bit
        return self.band + 1 - 2 * bit, self.batch

    def along_z(self, step):
        other = lax.rem(self.z + step, Z_COUNT)
        return other, (other * 2 + self.bits["y"], self.batch)


Z_COUNT = 4


def greet(others):
    barrier = pltpu.get_barrier_semaphore()
    for other in others:
        pl.semaphore_signal(barrier, inc=1, device_id=other, device_id_type=pl.DeviceIdType.MESH)
    pl.semaphore_wait(barrier, len(others))


class Total:
    def __init__(self, place, order, sends, recvs):
        self.place = place
        self.order = order
        self.sends, self.recvs = sends, recvs
        self.core = place.bits["core"]
        if order is not None:
            self.first, self.second = (place.bits[axis] for axis in order)

    def give(self, step, source, target, other):
        send(source, target, self.sends.at[step], self.recvs.at[step], *other)

    def took(self, step, ref):
        await_bytes(ref, self.recvs.at[step])
        await_bytes(ref, self.sends.at[step])

    def add(self, ref, rows, part):
        ref[rows] = (ref[rows].astype(F32) + part.astype(F32)).astype(BF16)

    def start_core(self, source, recv):
        self.give(0, source.at[1 - self.core], recv, self.place.across("core"))

    def end_core(self, held, recv):
        self.took(0, recv)
        held[...] = (held[...].astype(F32) + recv[...].astype(F32)).astype(BF16)

    def half_rows(self, held, level):
        rows = held.shape[0] // 2
        base = 0
        if level == 2:
            base, rows = self.first * rows, rows // 2
        bit = self.first if level == 1 else self.second
        keep = pl.ds(pl.multiple_of(base + bit * rows, rows), rows)
        away = pl.ds(pl.multiple_of(base + (1 - bit) * rows, rows), rows)
        return keep, away

    def start_half(self, level, held, recv):
        away = self.half_rows(held, level)[1]
        self.give(level, held.at[away], recv, self.place.across(self.order[level - 1]))

    def end_half(self, level, held, recv):
        self.took(level, recv)
        self.add(held, self.half_rows(held, level)[0], recv[...])

    def start_z(self, piece, recv):
        width = recv.shape[2]
        for step in range(1, Z_COUNT):
            index, other = self.place.along_z(step)
            lanes = pl.ds(pl.multiple_of(index * width, 128), width)
            self.give(3, piece.at[:, lanes], recv.at[step - 1], other)

    def z_lanes(self, width):
        return pl.ds(pl.multiple_of(self.place.z * width, 128), width)

    def end_z(self, piece, recv):
        self.took(3, recv)
        lanes = self.z_lanes(recv.shape[2])
        sums = piece[:, lanes].astype(F32)
        for step in range(Z_COUNT - 1):
            sums = sums + recv[step].astype(F32)
        piece[:, lanes] = sums.astype(BF16)

    def own_copy(self, piece, target, width, sem):
        lanes = self.z_lanes(width)
        return pltpu.make_async_copy(piece.at[:, lanes], target.at[:, lanes], sem)

    def start_z_back(self, piece, target, width, sem):
        lanes = self.z_lanes(width)
        for step in range(1, Z_COUNT):
            _, other = self.place.along_z(step)
            self.give(4, piece.at[:, lanes], target.at[:, lanes], other)
        self.own_copy(piece, target, width, sem).start()

    def end_z_back(self, piece, target, width, sem):
        self.took(4, target.at[:, pl.ds(0, (Z_COUNT - 1) * width)])
        self.own_copy(piece, target, width, sem).wait()

    def around(self):
        found = []
        for step in range(1, 4 * Z_COUNT):
            x = lax.rem(self.place.bits["x"] + step // 2 % 2, 2)
            y = lax.rem(self.place.bits["y"] + step % 2, 2)
            z = lax.rem(self.place.z + step // 4, Z_COUNT)
            found.append((2 * x + y, z, (2 * z + y, 2 * x + self.core)))
        return found

    def tile(self, ref, base, quarter, z, shape):
        rows = pl.ds(pl.multiple_of(base + quarter * shape[0], shape[0]), shape[0])
        return ref.at[rows, pl.ds(pl.multiple_of(z * shape[1], 128), shape[1])]

    def start_around(self, held, recv):
        for i, (quarter, z, other) in enumerate(self.around()):
            self.give(1, self.tile(held, 0, quarter, z, recv.shape[1:]), recv.at[i], other)

    def own_tile(self, ref, base, shape):
        return self.tile(ref, base, 2 * self.place.bits["x"] + self.place.bits["y"], self.place.z, shape)

    def end_around(self, held, recv):
        self.took(1, recv)
        own = self.own_tile(held, 0, recv.shape[1:])
        sums = own[...].astype(F32)
        for i in range(recv.shape[0]):
            sums = sums + recv[i].astype(F32)
        own[...] = sums.astype(BF16)

    def start_around_back(self, held, recv, out, sem):
        shape = recv.shape[1:]
        own = self.own_tile(held, 0, shape)
        target = self.own_tile(out, self.core * (out.shape[0] // 2), shape)
        for _, _, other in self.around():
            self.give(2, own, target, other)
        pltpu.make_async_copy(own, target, sem).start()

    def end_around_back(self, held, recv, out, sem):
        shape = recv.shape[1:]
        self.took(2, recv)
        target = self.own_tile(out, self.core * (out.shape[0] // 2), shape)
        pltpu.make_async_copy(self.own_tile(held, 0, shape), target, sem).wait()

    def back_rows(self, out, level):
        rows = out.shape[0] // 2
        base = self.core * rows
        if level >= 1:
            rows = rows // 2
            base = base + self.first * rows
        if level >= 2:
            rows = rows // 2
            base = base + self.second * rows
        return pl.ds(pl.multiple_of(base, rows), rows)

    def start_back(self, level, out, source=None):
        rows = self.back_rows(out, level)
        axis = "core" if level == 0 else self.order[level - 1]
        self.give(7 - level, out.at[rows] if source is None else source, out.at[rows], self.place.across(axis))

    def end_back(self, level, out):
        self.took(7 - level, out.at[self.back_rows(out, level)])


TOTAL_STEPS = 8


def time_forward_kernel(
    heads,
    batch_count,
    band_count,
    act_in,
    cot_in,
    count_ref,
    g1_ref,
    g2_ref,
    wgt_ref,
    wp_ref,
    wo_ref,
    w1_ref,
    w2_ref,
    band_wp_ref,
    band_wo_ref,
    band_w1_ref,
    band_w2_ref,
    band_rows,
    band_cot,
    rows_ref,
    n_ref,
    q_ref,
    k_ref,
    v_ref,
    p_ref,
    linv_ref,
    gate_ref,
    att_ref,
    mixed_ref,
    mid_ref,
    nf_ref,
    act_ref,
    slope_ref,
    band_wpt_ref,
    band_wot_ref,
    band_w1t_ref,
    band_w2t_ref,
    cos_ref,
    sin_ref,
    xt_ref,
    x_ref,
    result_ref,
    wpt_ref,
    wot_ref,
    w1t_ref,
    w2t_ref,
    row_send,
    row_recv,
    cot_send,
    cot_recv,
    result_send,
    result_recv,
    local_sem,
):
    slot, head = pl.program_id(0), pl.program_id(1)
    slots = pl.num_programs(0)
    slot_dev = cot_in.shape[0]
    frames, model = rows_ref.shape[1:]
    inner = q_ref.shape[1]
    size = inner // heads
    my_band, my_batch = lax.axis_index("band"), lax.axis_index("batch")
    frame_dev = frames // batch_count
    piece = frame_dev // band_count
    own_rows = pl.ds(pl.multiple_of(my_batch * frame_dev, frame_dev), frame_dev)
    held = x_ref.shape[0]
    frame_index = lax.broadcasted_iota(jnp.int32, (1, frames), 1)

    def neighbour(i):
        core, x = lax.rem(my_batch, 2), my_batch // 2
        return lax.rem(x + i // 2, 2) * 2 + lax.rem(core + lax.rem(i, 2), 2)

    def own_row_copy(j):
        return pltpu.make_async_copy(
            act_in.at[batch_count * j + my_batch], x_ref.at[j, own_rows], local_sem.at[j]
        )

    def own_cot_copy():
        return pltpu.make_async_copy(
            cot_in.at[:, pl.ds(pl.multiple_of(my_band * piece, piece), piece)],
            band_cot.at[pl.ds(my_band * slot_dev, slot_dev)],
            local_sem.at[held],
        )

    @pl.when((slot == 0) & (head == 0))
    def start():
        greet_all(band_count, batch_count)
        for j in range(held):
            for i in range(1, batch_count):
                other = neighbour(i)
                send(
                    act_in.at[batch_count * j + other],
                    x_ref.at[j, own_rows],
                    row_send,
                    row_recv.at[j, i],
                    my_band,
                    other,
                )
            own_row_copy(j).start()

        def send_cot(i, carry):
            other = lax.rem(my_band + i, band_count)
            send(
                cot_in.at[:, pl.ds(pl.multiple_of(other * piece, piece), piece)],
                band_cot.at[pl.ds(my_band * slot_dev, slot_dev)],
                cot_send,
                cot_recv,
                other,
                my_batch,
            )
            return carry

        lax.fori_loop(1, band_count, send_cot, 0)
        own_cot_copy().start()
        cos_ref[...], sin_ref[...] = rotary_rows(frame_index.astype(F32), size // 2)
        wpt_ref[...] = flipped(wp_ref)
        wot_ref[...] = flipped(wo_ref)
        w1t_ref[...] = flipped(w1_ref)
        w2t_ref[...] = flipped(w2_ref)
        band_wpt_ref[...] = flipped(band_wp_ref)
        band_wot_ref[...] = flipped(band_wo_ref)
        band_w1t_ref[...] = flipped(band_w1_ref)
        band_w2t_ref[...] = flipped(band_w2_ref)

    @pl.when(head == 0)
    def before():
        gain = column(g1_ref)

        def block(i, carry):
            at = pl.ds(pl.multiple_of(neighbour(i) * BLOCK, BLOCK), BLOCK)

            @pl.when(i == 0)
            def own():
                for j in range(held):

                    @pl.when(slot == j)
                    def kept():
                        own_row_copy(j).wait()

            @pl.when(i > 0)
            def arrived():
                await_bytes(x_ref.at[slot, at], row_recv.at[slot, i])

            held_rows = x_ref[slot, at, :]
            rows_ref[0, at, :] = held_rows
            rows = held_rows.astype(F32).T
            xt_ref[:, at] = rows
            normed = norm_forward(rows, gain)
            n_ref[0, :, at] = normed
            queries, keys, values = project_block(
                normed, wpt_ref, cos_ref[:, at], sin_ref[:, at], inner, LOG2E * size**-0.5
            )
            q_ref[0, :, at] = queries
            k_ref[0, :, at] = keys
            v_ref[0, :, at] = values
            gate_ref[0, :, at] = dg(wgt_ref[...], normed, NN)
            return carry

        lax.fori_loop(0, frames // BLOCK, block, 0, unroll=1)

    at_head = pl.ds(pl.multiple_of(head * size, size), size)
    ones = jnp.ones((1, frames), F32)
    queries = jnp.concatenate([q_ref[0, at_head, :], extra_rows([ones], frames)], axis=0)
    keys = jnp.concatenate([k_ref[0, at_head, :], extra_rows([jnp.where(frame_index < count_ref[0], 0.0, NEG_FILL)], frames)], axis=0)
    values = jnp.concatenate([v_ref[0, at_head, :], extra_rows([ones], frames)], axis=0)
    scores = dg(keys, queries, TN)
    weights = jnp.exp2(scores - jnp.max(scores, axis=0, keepdims=True)).astype(BF16)
    p_ref[0, 0] = weights
    sums = dg(values, weights, NN)
    inverse = 1.0 / sums[size : size + 1]
    attended = sums[:size] * inverse
    linv_ref[0, pl.ds(head, 1), :] = inverse
    att_ref[0, at_head, :] = attended
    gate = jax.nn.sigmoid(gate_ref[0, pl.ds(head, 1), :])
    mixed_ref[0, at_head, :] = (attended * gate).astype(BF16)

    @pl.when(head == heads - 1)
    def after():
        gain = column(g2_ref)
        to_slot = my_band * slot_dev + batch_count * slot + my_batch

        def block(i, carry):
            at = pl.ds(pl.multiple_of(i * BLOCK, BLOCK), BLOCK)
            middle = xt_ref[:, at] + dg(wot_ref[...], mixed_ref[0, :, at], NN)
            mid_ref[0, :, at] = middle
            normed = norm_forward(middle, gain)
            nf_ref[0, :, at] = normed
            result = feed_forward(
                middle, normed, w1t_ref, w2t_ref, act_ref.at[0, :, at], slope_ref.at[0, :, at]
            )
            result_ref[slot, at, :] = result.T.astype(BF16)

            def send_result(j, carry):
                other = lax.rem(my_band + j, band_count)
                source = result_ref.at[slot, pl.ds(pl.multiple_of(i * frame_dev + other * piece, piece), piece)]
                mine = (other == my_band) & (i == my_batch)

                @pl.when(mine)
                def keep():
                    pltpu.make_async_copy(source, band_rows.at[to_slot], local_sem.at[held + 1]).start()

                @pl.when(jnp.logical_not(mine))
                def give():
                    send(source, band_rows.at[to_slot], result_send, result_recv, other, i)

                return carry

            lax.fori_loop(1, band_count + 1, send_result, 0)
            return carry

        lax.fori_loop(0, frames // BLOCK, block, 0, unroll=1)

    @pl.when((slot == slots - 1) & (head == heads - 1))
    def finish():
        others = held * (band_count * batch_count - 1)
        others_cot = (band_count - 1) * slot_dev
        others_rows = (batch_count - 1) * frame_dev
        await_bytes(band_cot.at[pl.ds(0, others_cot)], cot_recv)
        await_bytes(band_cot.at[pl.ds(0, others_cot)], cot_send)
        own_cot_copy().wait()
        await_bytes(x_ref.at[:, pl.ds(0, others_rows)], row_send)
        await_bytes(band_rows.at[pl.ds(0, others)], result_send)
        await_bytes(band_rows.at[pl.ds(0, held)], local_sem.at[held + 1])
        await_bytes(band_rows.at[pl.ds(0, others)], result_recv)


def cost(flops, exps=0, moved=0):
    return pl.CostEstimate(flops=int(flops), bytes_accessed=int(moved), transcendentals=int(exps))


def whole_spec(array):
    nd = array.ndim
    return pl.BlockSpec(array.shape, lambda *ids: (0,) * nd, pipeline_mode=pl.Buffered(1))


def time_forward(activations, cotangent, counts, g1, g2, params, band_params, band_count, batch_count):
    wp, wgt, wo, w1, w2 = params
    bwp, _, bwo, bw1, bw2 = band_params
    slot_dev, frame_dev, model = activations.shape
    slots, frames = slot_dev // batch_count, frame_dev * batch_count
    heads, inner, hidden = wgt.shape[0], wo.shape[0], w1.shape[1]
    piece = frame_dev // band_count

    def per_slot(*shape):
        return pl.BlockSpec((1,) + shape, lambda s, h: (s,) + (0,) * len(shape))

    outs = [
        ((frames, model), BF16),
        ((model, frames), BF16),
        ((inner, frames), BF16),
        ((inner, frames), BF16),
        ((inner, frames), BF16),
        None,
        ((heads, frames), F32),
        ((heads, frames), F32),
        ((inner, frames), F32),
        ((inner, frames), BF16),
        ((model, frames), F32),
        ((model, frames), BF16),
        ((hidden, frames), BF16),
        ((hidden, frames), BF16),
    ]
    flips = [(w.shape[1], w.shape[0]) for w in (bwp, bwo, bw1, bw2)]
    own_flips = [(w.shape[1], w.shape[0]) for w in (wp, wo, w1, w2)]
    exchanged = jax.ShapeDtypeStruct((slot_dev * band_count, piece, model), BF16)
    anywhere = pl.BlockSpec(memory_space=pl.ANY)
    shapes, specs = [exchanged, exchanged], [anywhere, anywhere]
    for entry in outs:
        if entry is None:
            shapes.append(jax.ShapeDtypeStruct((slots, heads, frames, frames), BF16))
            specs.append(pl.BlockSpec((1, 1, frames, frames), lambda s, h: (s, h, 0, 0)))
        else:
            shapes.append(jax.ShapeDtypeStruct((slots,) + entry[0], entry[1]))
            specs.append(per_slot(*entry[0]))
    for shape in flips:
        shapes.append(jax.ShapeDtypeStruct(shape, BF16))
        specs.append(pl.BlockSpec(shape, lambda s, h: (0, 0), pipeline_mode=pl.Buffered(1)))
    consts = (g1, g2, wgt, wp, wo, w1, w2, bwp, bwo, bw1, bw2)
    half = inner // heads // 2
    for _ in range(2):
        shapes.append(jax.ShapeDtypeStruct((half, frames), F32))
        specs.append(pl.BlockSpec((half, frames), lambda s, h: (0, 0)))
    dma = pltpu.SemaphoreType.DMA
    return pl.pallas_call(
        lambda *refs: time_forward_kernel(heads, batch_count, band_count, *refs),
        grid=(slots, heads),
        out_shape=shapes,
        in_specs=[anywhere, anywhere, pl.BlockSpec(memory_space=pltpu.SMEM)] + [whole_spec(c) for c in consts],
        out_specs=specs,
        scratch_shapes=[
            pltpu.VMEM((model, frames), F32),
            pltpu.VMEM((slots, frames, model), BF16),
            pltpu.VMEM((slots, frames, model), BF16),
        ]
        + [pltpu.VMEM(shape, BF16) for shape in own_flips]
        + [dma, dma((slots, batch_count)), dma, dma, dma, dma, dma((slots + 2,))],
        compiler_params=pltpu.CompilerParams(
            vmem_limit_bytes=VMEM_BYTES, collective_id=0, has_side_effects=True
        ),
        cost_estimate=cost(2.0e6 * 4 * slots * frames, 2 * slots * heads * frames * frames, 60e6),
        name="time_forward",
    )(activations, cotangent, counts, *consts)


def ffn_backward(grad, slope, middle, gain, w1_ref, w2_ref, dg2_ref):
    branch = grad.astype(BF16)
    d_hidden = (dg(w2_ref[...], branch, NN) * slope.astype(F32)).astype(BF16)
    d_normed = dg(w1_ref[...], d_hidden, NN)
    d_rows, terms = norm_backward(middle, gain, d_normed)
    dg2_ref[...] += jnp.sum(terms, axis=1, keepdims=True)
    return grad + d_rows, branch, d_hidden


def add_ffn_sums(dw1_ref, dw2t_ref, branch, act, normed, d_hidden):
    dw2t_ref[...] += dg(branch, act, NT)
    dw1_ref[...] += dg(normed, d_hidden, NT)


def head_backward(d_mixed, attended, gate_logit, inverse):
    gate = jax.nn.sigmoid(gate_logit)
    d_logit = jnp.sum(d_mixed * attended, axis=0, keepdims=True) * gate * (1.0 - gate)
    d_att = (d_mixed * (gate * inverse)).astype(BF16)
    minus = -jnp.sum(d_att.astype(F32) * attended, axis=0, keepdims=True)
    return d_att, minus, d_logit


def scores_backward(queries, keys, values, weights, d_att, minus, cos, sin, scale):
    width = queries.shape[1]
    ones = jnp.ones((1, width), F32)
    d_weights = dg(
        jnp.concatenate([values, extra_rows([ones, ones, ones], width)], axis=0),
        jnp.concatenate([d_att, extra_rows(list(three_parts(minus)), width)], axis=0),
        TN,
    )
    d_scores = (weights.astype(F32) * d_weights).astype(BF16)
    d_values = dg(d_att, weights, NT)
    d_queries = dg(keys, d_scores, NN) * scale
    d_keys = dg(queries, d_scores, NT) * (1.0 / LOG2E)
    return turn(d_queries, cos, -sin), turn(d_keys, cos, -sin), d_values


def time_ffn_backward_kernel(
    heads,
    grad_ref,
    act_ref,
    slope_ref,
    nf_ref,
    mid_ref,
    mixed_ref,
    att_ref,
    gate_ref,
    linv_ref,
    g2_ref,
    w1_ref,
    w2_ref,
    wo_ref,
    half_refs,
    dmid_ref,
    datt_ref,
    minus_ref,
    dlogit_ref,
    sums_refs,
    dg2_out,
    part_refs,
    dw1_ref,
    dw2t_ref,
    dwot_ref,
    dg2_ref,
    held_refs,
    half_recvs,
    z_recvs,
    sends,
    recvs,
    local_sem,
):
    place = Place()
    totals = [Total(place, order, sends.at[i], recvs.at[i]) for i, order in enumerate(BAND_ORDERS)]
    early = len(z_recvs)
    work = list(zip(totals, half_refs, held_refs, half_recvs))

    def half_copy(i):
        return pltpu.make_async_copy(half_refs[i], held_refs[i], local_sem.at[i])

    def part_copy(i):
        rows = totals[i].half_rows(held_refs[i], 2)[0]
        return pltpu.make_async_copy(held_refs[i].at[rows], part_refs[i], local_sem.at[len(totals) + i])

    step = pl.program_id(0) * pl.num_programs(1) + pl.program_id(1)
    last = pl.num_programs(0) * pl.num_programs(1) - 1
    size = wo_ref.shape[0] // heads

    @pl.when(step == 0)
    def clear():
        for ref in (dw1_ref, dw2t_ref, dwot_ref, dg2_ref):
            ref[...] = jnp.zeros_like(ref)
        greet([place.across("x"), place.across("y")] + [place.along_z(i)[1] for i in range(1, Z_COUNT)])
        for i, (total, halves, held, recv) in enumerate(work):
            half_copy(i).start()
            total.start_half(1, halves, recv[0])

    def eighth(i):
        return held_refs[i].at[totals[i].half_rows(held_refs[i], 2)[0]]

    @pl.when(step == last - 1)
    def first_half():
        for i, (total, halves, held, recv) in list(enumerate(work))[:early]:
            half_copy(i).wait()
            total.end_half(1, held, recv[0])
            total.start_half(2, held, recv[1])

    @pl.when(step == last)
    def second_half():
        for i, (total, halves, held, recv) in list(enumerate(work))[early:]:
            half_copy(i).wait()
            total.end_half(1, held, recv[0])
            total.start_half(2, held, recv[1])
        for i, (total, halves, held, recv) in list(enumerate(work))[:early]:
            total.end_half(2, held, recv[1])
            total.start_z(eighth(i), z_recvs[i])

    slot = pl.program_id(0)
    chunks, parts, rows, model = grad_ref.shape
    slots = pl.num_programs(0)
    taken = rows // slots
    both = grad_ref[...].astype(F32).reshape(chunks * parts, slots, taken, model)
    grad = both[:, 0]
    for j in range(1, slots):
        grad = jnp.where(slot == j, both[:, j], grad)
    grad = grad.reshape(chunks * parts * taken, model).T
    d_middle, branch, d_hidden = ffn_backward(
        grad, slope_ref[0], mid_ref[0], column(g2_ref), w1_ref, w2_ref, dg2_ref
    )
    add_ffn_sums(dw1_ref, dw2t_ref, branch, act_ref[0], nf_ref[0], d_hidden)
    dmid_ref[0] = d_middle
    branch = d_middle.astype(BF16)
    dwot_ref[...] += dg(branch, mixed_ref[0], NT)
    d_mixed = dg(wo_ref[...], branch, NN)
    logits, minuses = [], []
    for head in range(heads):
        at = slice(head * size, (head + 1) * size)
        d_att, minus, d_logit = head_backward(
            d_mixed[at], att_ref[0, at], gate_ref[0, head : head + 1], linv_ref[0, head : head + 1]
        )
        datt_ref[0, at] = d_att
        minuses.append(minus)
        logits.append(d_logit)
    minus_ref[0] = jnp.concatenate(minuses, axis=0)
    dlogit_ref[0] = jnp.concatenate(logits, axis=0)

    @pl.when(step == last)
    def finish():
        for sums, ref in zip(sums_refs, (dw2t_ref, dw1_ref, dwot_ref)):
            lay_halves(sums, 0, ref)
        dg2_out[...] = dg2_ref[...]
        for i, (total, halves, held, recv) in list(enumerate(work))[early:]:
            total.end_half(2, held, recv[1])
            part_copy(i).start()
        for i, (total, halves, held, recv) in list(enumerate(work))[:early]:
            total.end_z(eighth(i), z_recvs[i])
            part_copy(i).start()
        for i in range(len(work)):
            part_copy(i).wait()


def narrow_tile(parts, rows):
    used = sum(part.shape[1] for part in parts)
    return jnp.concatenate(list(parts) + [jnp.zeros((rows, 128 - used), F32)], axis=1)


def lay_halves(target, at, ref):
    rows, width = ref.shape
    for half in range(2):
        target[half, :, at : at + width] = ref[half * rows // 2 : (half + 1) * rows // 2].astype(BF16)


XY, YX = ("x", "y"), ("y", "x")
BAND_ORDERS = (YX, XY, YX, XY)
BAND_EARLY = 2
FFN_ORDERS = (YX, XY, YX)
PAIR_ORDERS = (YX, YX, YX, None)


def time_ffn_backward(grad, act, slope, nf, mid, mixed, att, gate, linv, g2, w1, w2, wo, halves_in):
    slots, model, frames = mid.shape
    heads = gate.shape[1]
    inner, hidden = wo.shape[0], w1.shape[1]
    chunks, parts, _, _ = grad.shape
    tokens = frames // 2

    def cut(rows):
        return pl.BlockSpec((1, rows, tokens), lambda s, c: (s, 0, c))

    def whole(*shape):
        return pl.BlockSpec(shape, lambda s, c: (0,) * len(shape))

    consts = (g2, w1, w2, wo)
    anywhere = pl.BlockSpec(memory_space=pl.ANY)
    halves = [(2, model // 2, width) for width in (hidden, hidden, inner)]
    widths = [a.shape[1] for a in halves_in]
    dma = pltpu.SemaphoreType.DMA
    return pl.pallas_call(
        lambda *refs: time_ffn_backward_kernel(heads, *refs),
        grid=(slots, frames // tokens),
        out_shape=(
            jax.ShapeDtypeStruct((slots, model, frames), F32),
            jax.ShapeDtypeStruct((slots, inner, frames), BF16),
            jax.ShapeDtypeStruct((slots, heads, frames), F32),
            jax.ShapeDtypeStruct((slots, heads, frames), F32),
            [jax.ShapeDtypeStruct(shape, BF16) for shape in halves],
            jax.ShapeDtypeStruct((model, 1), F32),
            [jax.ShapeDtypeStruct((model // 8, width), BF16) for width in widths],
        ),
        in_specs=[pl.BlockSpec((chunks // 2,) + grad.shape[1:], lambda s, c: (c, 0, 0, 0))]
        + [cut(a.shape[1]) for a in (act, slope, nf, mid, mixed, att, gate, linv)]
        + [whole_spec(c) for c in consts]
        + [[anywhere for _ in widths]],
        out_specs=(
            cut(model),
            cut(inner),
            cut(heads),
            cut(heads),
            [whole(*shape) for shape in halves],
            whole(model, 1),
            [anywhere for _ in widths],
        ),
        scratch_shapes=[
            pltpu.VMEM((model, hidden), F32),
            pltpu.VMEM((model, hidden), F32),
            pltpu.VMEM((model, inner), F32),
            pltpu.VMEM((model, 1), F32),
            [pltpu.VMEM((model // 2, width), BF16) for width in widths],
            [
                [pltpu.VMEM((rows, width), BF16) for rows in (model // 4, model // 8)]
                for width in widths
            ],
            [pltpu.VMEM((Z_COUNT - 1, model // 8, width // Z_COUNT), BF16) for width in widths[:BAND_EARLY]],
            dma((len(widths), TOTAL_STEPS)),
            dma((len(widths), TOTAL_STEPS)),
            dma((2 * len(widths),)),
        ],
        compiler_params=pltpu.CompilerParams(
            vmem_limit_bytes=VMEM_BYTES, collective_id=2, has_side_effects=True
        ),
        cost_estimate=cost(8.0e6 * slots * frames, 0, 30e6),
        name="time_ffn_backward",
    )(grad, act, slope, nf, mid, mixed, att, gate, linv, *consts, list(halves_in))


BAND_PLACES = ((0, 4, 7, 11, 13), (0, 4, 7, 12, 14), (0, 4, 7, 11, 16, 18), (0, 5, 8, 12, 16, 18))
FFN_PLACES = ((0, 1, 5, 8, 12, 15, 18, 24, 25), (0, 2, 6, 10, 13, 16, 20, 24, 25), (0, 2, 6, 9, 12, 15, 18, 22, 24))
PAIR_PLACES = (
    (4, 5, 8, 12, 15, 18, 22, 24, 25),
    (8, 9, 12, 15, 17, 20, 23, 24, 25),
    (12, 13, 15, 18, 21, 24, 25, 26, 27),
    (16, 17, 21, 24, 25),
)


def time_attention_backward_kernel(
    heads,
    slots,
    batch_count,
    p_ref,
    q_ref,
    k_ref,
    v_ref,
    datt_ref,
    minus_ref,
    x_ref,
    dmid_ref,
    logit_block_ref,
    n_ref,
    dlogit_ref,
    cos_ref,
    sin_ref,
    g1_ref,
    wp_ref,
    wgt_ref,
    narrow_ref,
    dg2_ref,
    part_refs,
    ffn_refs,
    grad_out,
    band_outs,
    ffn_outs,
    pair_outs,
    dproj_ref,
    wp_turned_ref,
    grad_buf,
    piece_refs,
    band_recvs,
    held_refs,
    ffn_recvs,
    pair_refs,
    pair_recvs,
    around_recv,
    band_sems,
    ffn_sems,
    pair_sems,
    grad_sems,
    local_sem,
):
    place = Place()
    step = pl.program_id(0)
    steps = heads * slots
    head, slot = step // slots, lax.rem(step, slots)
    size, frames = q_ref.shape[1:]
    model = n_ref.shape[1]
    inner = heads * size
    pairs = heads // 2
    pair_rows = 6 * size
    blocks = frames // BLOCK
    last = pl.num_programs(0) - 1
    my_band, my_batch = place.band, place.batch

    bands = [Total(place, order, band_sems[0].at[i], band_sems[1].at[i]) for i, order in enumerate(BAND_ORDERS)]
    ffns = [Total(place, order, ffn_sems[0].at[i], ffn_sems[1].at[i]) for i, order in enumerate(FFN_ORDERS)]
    own = [
        Total(place, PAIR_ORDERS[i], pair_sems[0].at[i], pair_sems[1].at[i]) for i in range(pairs)
    ]

    def half_copy(i):
        return pltpu.make_async_copy(ffn_refs[i].at[place.bits["core"]], held_refs[i], local_sem.at[len(bands) + i])

    def eighth(total, held):
        return held.at[total.half_rows(held, 2)[0]]

    def all_steps(total, source, held, recvs, out, sem):
        width = recvs[3].shape[2]

        def back_region():
            return out.at[total.back_rows(out, 2)]

        def s0():
            total.start_core(source, recvs[0])

        def s1():
            total.end_core(held, recvs[0])
            total.start_half(1, held, recvs[1])

        def s2():
            total.end_half(1, held, recvs[1])
            total.start_half(2, held, recvs[2])

        def s3():
            total.end_half(2, held, recvs[2])
            total.start_z(eighth(total, held), recvs[3])

        def s4():
            total.end_z(eighth(total, held), recvs[3])
            total.start_z_back(eighth(total, held), back_region(), width, sem)

        def s5():
            total.end_z_back(eighth(total, held), back_region(), width, sem)
            total.start_back(2, out)

        def s6():
            total.end_back(2, out)
            total.start_back(1, out)

        def s7():
            total.end_back(1, out)
            total.start_back(0, out)

        def s8():
            total.end_back(0, out)

        return [s0, s1, s2, s3, s4, s5, s6, s7, s8]

    plan = {}

    def at_step(index, action):
        plan.setdefault(index, []).append(action)

    def enter():
        other_x = place.across("x")[1] // 2
        diagonal = (my_band, 2 * other_x + 1 - place.bits["core"])
        chips = [other for _, _, other in own[-1].around()]
        greet(chips + [place.across("core"), diagonal])
        for i in range(len(ffns)):
            half_copy(i).start()

    tail = steps + slots * blocks
    at_step(0, enter)

    def schedule(actions, places):
        for at, action in zip(places, actions):
            at_step(at, action)

    for i in range(len(bands)):
        out = band_outs[i]
        region = out.at[bands[i].back_rows(out, 2)]
        quarter = band_outs[i].shape[1] // Z_COUNT

        def z_begin(i=i):
            piece_refs[i][...] = part_refs[i][...]
            if i >= BAND_EARLY:
                bands[i].start_z(piece_refs[i], band_recvs[i - BAND_EARLY])

        def z_turn(i=i, region=region, quarter=quarter):
            if i >= BAND_EARLY:
                bands[i].end_z(piece_refs[i], band_recvs[i - BAND_EARLY])
            bands[i].start_z_back(piece_refs[i], region, quarter, local_sem.at[i])

        def z_end(i=i, region=region, quarter=quarter, out=out):
            bands[i].end_z_back(piece_refs[i], region, quarter, local_sem.at[i])
            bands[i].start_back(2, out)

        def back_two(i=i, out=out):
            bands[i].end_back(2, out)
            bands[i].start_back(1, out)

        def back_one(i=i, out=out):
            bands[i].end_back(1, out)
            bands[i].start_back(0, out)

        actions = [z_begin, z_turn, z_end, back_two, back_one, lambda i=i, out=out: bands[i].end_back(0, out)]
        if i < BAND_EARLY:
            at_step(0, z_begin)
            actions = actions[1:]
        schedule(actions, BAND_PLACES[i])
    ffn_at = len(bands) + len(ffns)
    for i in range(len(ffns)):
        sem = local_sem.at[ffn_at + i]
        actions = all_steps(ffns[i], ffn_refs[i], held_refs[i], ffn_recvs[i], ffn_outs[i], sem)
        at_step(FFN_PLACES[i][1], lambda i=i: half_copy(i).wait())
        schedule(actions, FFN_PLACES[i])
    pair_at = ffn_at + len(ffns)

    def around_steps(total, source, held, recv, out, sem):
        def s0():
            total.start_core(source, recv[0])

        def s1():
            total.end_core(held, recv[0])
            total.start_around(held, recv[1])

        def s2():
            total.end_around(held, recv[1])
            total.start_around_back(held, recv[1], out, sem)

        def s3():
            total.end_around_back(held, recv[1], out, sem)
            total.start_back(0, out)

        def s4():
            total.end_back(0, out)

        return [s0, s1, s2, s3, s4]

    for i in range(pairs):
        source, held = pair_refs.at[i], pair_refs.at[i, place.bits["core"]]
        out, sem = pair_outs.at[i], local_sem.at[pair_at + i]
        recv = [ref.at[i] for ref in pair_recvs]
        if PAIR_ORDERS[i] is None:
            actions = around_steps(own[i], source, held, [recv[0], around_recv], out, sem)
        else:
            actions = all_steps(own[i], source, held, recv, out, sem)
        schedule(actions, PAIR_PLACES[i])

    for index in sorted(plan):
        if index < tail:

            @pl.when(step == index)
            def work(index=index):
                for action in plan[index]:
                    action()

    @pl.when(step < steps)
    def attention():
        d_queries, d_keys, d_values = scores_backward(
            q_ref[0],
            k_ref[0],
            v_ref[0],
            p_ref[0, 0],
            datt_ref[0],
            minus_ref[0, pl.ds(head, 1), :],
            cos_ref[...],
            sin_ref[...],
            size**-0.5,
        )
        start = pl.multiple_of((head // 2) * pair_rows + lax.rem(head, 2) * size, size)
        dproj_ref[slot, pl.ds(start, size), :] = d_queries.astype(BF16)
        dproj_ref[slot, pl.ds(start + 2 * size, size), :] = d_keys.astype(BF16)
        dproj_ref[slot, pl.ds(start + 4 * size, size), :] = d_values.astype(BF16)

    @pl.when((step < steps) & (lax.rem(step, 2 * slots) == 2 * slots - 1))
    def pair_done():
        pair = head // 2
        rows = pl.ds(pl.multiple_of(pair * pair_rows, pair_rows), pair_rows)
        sums = dg(n_ref[0], dproj_ref[0, rows, :], NT)
        for j in range(1, slots):
            sums = sums + dg(n_ref[j], dproj_ref[j, rows, :], NT)
        for half in range(2):
            at = slice(half * model // 2, (half + 1) * model // 2)
            pair_refs[pair, half, :, 0:pair_rows] = sums[at].astype(BF16)

    @pl.when(step == 2 * slots - 1)
    def narrow_done():
        gates = 0.0
        for j in range(slots):
            logit = jnp.concatenate([dlogit_ref[j], jnp.zeros_like(dlogit_ref[j])], axis=0).astype(BF16)
            gates = gates + dg(n_ref[j], logit, NT)[:, :heads]
        tile = narrow_tile([narrow_ref[:, : heads + 2], gates, dg2_ref[...]], model)
        for half in range(2):
            at = slice(half * model // 2, (half + 1) * model // 2)
            pair_refs[0, half, :, pair_rows:] = tile[at].astype(BF16)
            for i in range(1, pairs):
                pair_refs[i, half, :, pair_rows:] = jnp.zeros_like(tile[at]).astype(BF16)
        for pair in range(pairs):
            for part in range(3):
                to = pair * pair_rows + part * 2 * size
                source = part * inner + pair * 2 * size
                wp_turned_ref[:, to : to + 2 * size] = wp_ref[:, source : source + 2 * size]

    def message(index):
        j, i = index // blocks, lax.rem(index, blocks)
        source = grad_buf.at[index]
        target = grad_out.at[batch_count * j + my_batch]
        return i, source, target

    @pl.when(step >= steps)
    def rows_done():
        index = step - steps
        j, i = index // blocks, lax.rem(index, blocks)
        at = pl.ds(pl.multiple_of(i * BLOCK, BLOCK), BLOCK)
        logit = logit_block_ref[0].astype(BF16)
        d_normed = dg(wp_turned_ref[...], dproj_ref[j, :, at], NN) + dg(wgt_ref[...], logit, TN)
        d_rows, _ = norm_backward(x_ref[0].astype(F32).T, column(g1_ref), d_normed)
        grad_buf[index] = (dmid_ref[0] + d_rows).T.astype(BF16)
        i, source, target = message(index)

        @pl.when(i == my_batch)
        def keep():
            pltpu.make_async_copy(source, target, local_sem.at[pair_at + pairs]).start()

        @pl.when(i != my_batch)
        def give():
            send(source, target, grad_sems.at[0], grad_sems.at[1], my_band, i)

    @pl.when(step == last)
    def finish():
        for index in sorted(plan):
            if index >= tail:
                for action in plan[index]:
                    action()
        await_bytes(grad_buf.at[pl.ds(0, slots)], local_sem.at[pair_at + pairs])
        others = grad_buf.at[pl.ds(0, slots * (batch_count - 1))]
        await_bytes(others, grad_sems.at[0])
        await_bytes(others, grad_sems.at[1])


def time_attention_backward(
    p, q, k, v, datt, minus, dlogit, n, x, dmid, cos, sin, g1, wp, wgt, narrow, dg2, parts, ffn_sums, batch_count
):
    slots, inner, frames = q.shape
    heads = minus.shape[1]
    size = inner // heads
    model = n.shape[1]
    pairs = heads // 2
    steps = heads * slots
    blocks = frames // BLOCK

    def clamp(t):
        return jnp.minimum(t, steps - 1)

    def tail(t):
        return jnp.maximum(t - steps, 0)

    def per_head(rows, columns):
        return pl.BlockSpec((1, rows, columns), lambda t: (lax.rem(clamp(t), slots), clamp(t) // slots, 0))

    consts = (n, dlogit, cos, sin, g1, wp, wgt, narrow, dg2)
    anywhere = pl.BlockSpec(memory_space=pl.ANY)
    dma = pltpu.SemaphoreType.DMA
    widths = [a.shape[2] for a in ffn_sums]
    pair_width = 8 * size

    def recv_buffers(width, *lead):
        rows = model // 2
        shapes = [(rows, width), (rows // 2, width), (rows // 4, width), (Z_COUNT - 1, rows // 4, width // Z_COUNT)]
        return [pltpu.VMEM(lead + shape, BF16) for shape in shapes]

    return pl.pallas_call(
        lambda *refs: time_attention_backward_kernel(heads, slots, batch_count, *refs),
        grid=(steps + slots * blocks,),
        out_shape=(
            jax.ShapeDtypeStruct((batch_count * slots, BLOCK, model), BF16),
            [jax.ShapeDtypeStruct((model, a.shape[1]), BF16) for a in parts],
            [jax.ShapeDtypeStruct((model, width), BF16) for width in widths],
            jax.ShapeDtypeStruct((pairs, model, pair_width), BF16),
        ),
        in_specs=[
            pl.BlockSpec((1, 1, frames, frames), lambda t: (lax.rem(clamp(t), slots), clamp(t) // slots, 0, 0)),
            per_head(size, frames),
            per_head(size, frames),
            per_head(size, frames),
            per_head(size, frames),
            pl.BlockSpec((1, heads, frames), lambda t: (lax.rem(clamp(t), slots), 0, 0)),
            pl.BlockSpec((1, BLOCK, model), lambda t: (tail(t) // blocks, lax.rem(tail(t), blocks), 0)),
            pl.BlockSpec((1, model, BLOCK), lambda t: (tail(t) // blocks, 0, lax.rem(tail(t), blocks))),
            pl.BlockSpec((1, heads, BLOCK), lambda t: (tail(t) // blocks, 0, lax.rem(tail(t), blocks))),
        ]
        + [whole_spec(c) for c in consts]
        + [[whole_spec(a) for a in parts], [anywhere] * len(ffn_sums)],
        out_specs=(anywhere, [anywhere] * len(parts), [anywhere] * len(ffn_sums), anywhere),
        scratch_shapes=[
            pltpu.VMEM((slots, 3 * inner, frames), BF16),
            pltpu.VMEM((model, 3 * inner), BF16),
            pltpu.VMEM((slots * blocks, BLOCK, model), BF16),
            [pltpu.VMEM(a.shape, BF16) for a in parts],
            [pltpu.VMEM((Z_COUNT - 1, a.shape[0], a.shape[1] // Z_COUNT), BF16) for a in parts[BAND_EARLY:]],
            [pltpu.VMEM((model // 2, width), BF16) for width in widths],
            [recv_buffers(width) for width in widths],
            pltpu.VMEM((pairs, 2, model // 2, pair_width), BF16),
            recv_buffers(pair_width, pairs),
            pltpu.VMEM((4 * Z_COUNT - 1, model // 8, pair_width // Z_COUNT), BF16),
            [dma((len(parts), TOTAL_STEPS))] * 2,
            [dma((len(widths), TOTAL_STEPS))] * 2,
            [dma((pairs, TOTAL_STEPS)), dma((pairs, TOTAL_STEPS))],
            dma((2,)),
            dma((len(parts) + 2 * len(widths) + pairs + 1,)),
        ],
        compiler_params=pltpu.CompilerParams(
            vmem_limit_bytes=VMEM_BYTES, collective_id=3, has_side_effects=True
        ),
        cost_estimate=cost(20.0e6 * slots * frames, 0, 60e6),
        name="time_attention_backward",
    )(p, q, k, v, datt, minus, x, dmid, dlogit, *consts, list(parts), list(ffn_sums))


def finish_kernel(
    heads,
    grad_ref,
    bwp_ref,
    bw1_ref,
    bw2t_ref,
    bwot_ref,
    w1_ref,
    wot_ref,
    w2t_ref,
    pair_ref,
    first_pair_ref,
    wp_ref,
    wgt_ref,
    g1_ref,
    y_ref,
    y_out,
    grad_out,
    dg1_out,
    dwp_out,
    dwg_out,
    dwo_out,
    dg2_out,
    dw1_out,
    dw2_out,
    bg1_out,
    bwp_out,
    bwg_out,
    bwo_out,
    bg2_out,
    bw1_out,
    bw2_out,
    scaled_ref,
):
    pair = pl.program_id(0)
    inner = wp_ref.shape[1] // 3
    width = inner // pl.num_programs(0)
    pairs, bands, parts, rows, model = y_ref.shape
    split = y_ref[...].astype(F32).reshape(pairs, bands, parts, 2, rows // 2, model)
    for j in range(2):
        values = split[:, :, :, j].reshape(pairs, bands * parts * rows // 2, model)
        for i in range(pairs):
            y_out[2 * i + j] = values[i].astype(BF16)
    grad_out[...] = grad_ref[...].astype(F32)
    bwp_out[...] = bwp_ref[...].astype(F32)
    bw1_out[...] = bw1_ref[...].astype(F32)
    bw2_out[...] = bw2t_ref[...].astype(F32).T
    bwo_out[...] = bwot_ref[...].astype(F32).T
    dw1_out[...] = w1_ref[...].astype(F32)
    dw2_out[...] = w2t_ref[...].astype(F32).T
    dwo_out[...] = wot_ref[...].astype(F32).T

    @pl.when(pair == 0)
    def clear():
        scaled_ref[...] = jnp.zeros_like(scaled_ref)

    for part in range(3):
        at = pl.ds(pl.multiple_of(part * inner + pair * width, 128), width)
        values = pair_ref[0, :, part * width : (part + 1) * width].astype(F32)
        dwp_out[:, at] = values
        scaled_ref[...] += values * wp_ref[:, at].astype(F32)

    @pl.when(pair == pl.num_programs(0) - 1)
    def narrow():
        tile = first_pair_ref[0, :, 3 * width :].astype(F32)
        rows = tile.T
        bwg_out[...] = rows[:heads]
        bg1_out[...] = rows[heads]
        bg2_out[...] = rows[heads + 1]
        gates = tile[:, heads + 2 : 2 * heads + 2]
        dwg_out[...] = rows[heads + 2 : 2 * heads + 2]
        dg2_out[...] = rows[2 * heads + 2]
        sums = jnp.sum(scaled_ref[...], axis=1, keepdims=True)
        sums = sums + jnp.sum(gates * wgt_ref[...].astype(F32).T, axis=1, keepdims=True)
        dg1_out[...] = jnp.broadcast_to(sums, (sums.shape[0], 128)).T[0] / g1_ref[...].astype(F32)


def finish_sums(grads, y, band_sums, ffn_sums, pair_sums, g1, params):
    wp, wgt, wo, w1, w2 = params
    model, hidden = w1.shape
    inner, heads = wo.shape[0], wgt.shape[0]
    pairs = pair_sums.shape[0]
    split = hidden // pairs
    out_split = inner // pairs
    slot_dev, frame_dev, _ = grads.shape

    def lanes(width):
        return pl.BlockSpec((model, width), lambda i: (0, i))

    def whole(*shape):
        return pl.BlockSpec(shape, lambda i: (0,) * len(shape))

    def cut_rows(rows):
        return pl.BlockSpec((rows, model), lambda i: (i, 0))

    band_wp, band_w1, band_w2t, band_wot = band_sums
    time_w2t, time_w1, time_wot = ffn_sums
    grad_block = pl.BlockSpec((slot_dev // pairs, frame_dev, model), lambda i: (i, 0, 0))
    narrow = [((model,), whole(model)), ((heads, model), whole(heads, model))]
    per_layer = [
        narrow[0],
        ((model, 3 * inner), None),
        narrow[1],
        ((inner, model), cut_rows(out_split)),
        narrow[0],
        ((model, hidden), lanes(split)),
        ((hidden, model), cut_rows(split)),
    ]
    shapes, specs = [jax.ShapeDtypeStruct(grads.shape, BF16), jax.ShapeDtypeStruct(grads.shape, F32)], [grad_block] * 2
    y_block = pl.BlockSpec((y.shape[0] // pairs,) + y.shape[1:], lambda i: (i, 0, 0, 0, 0))
    for layer in range(2):
        for shape, spec in per_layer:
            shapes.append(jax.ShapeDtypeStruct(shape, F32))
            if spec is None:
                spec = whole(*shape) if layer == 0 else lanes(3 * inner // pairs)
            specs.append(spec)
    return pl.pallas_call(
        lambda *refs: finish_kernel(heads, *refs),
        grid=(pairs,),
        out_shape=shapes,
        in_specs=[
            grad_block,
            lanes(3 * inner // pairs),
            lanes(split),
            lanes(split),
            lanes(out_split),
            lanes(split),
            lanes(out_split),
            lanes(split),
            pl.BlockSpec((1, model, pair_sums.shape[2]), lambda i: (i, 0, 0)),
            pl.BlockSpec((1, model, pair_sums.shape[2]), lambda i: (0, 0, 0)),
            whole_spec(wp),
            whole_spec(wgt),
            whole_spec(g1),
            y_block,
        ],
        out_specs=specs,
        scratch_shapes=[pltpu.VMEM((model, inner // pairs), F32)],
        compiler_params=pltpu.CompilerParams(vmem_limit_bytes=VMEM_BYTES),
        name="finish_sums",
    )(
        grads,
        band_wp,
        band_w1,
        band_w2t,
        band_wot,
        time_w1,
        time_wot,
        time_w2t,
        pair_sums,
        pair_sums,
        wp,
        wgt,
        g1,
        y,
    )


def band_kernel(
    heads,
    batch_count,
    band_count,
    x_ref,
    cot_ref,
    count_ref,
    slots_ref,
    g1_ref,
    g2_ref,
    wgt_ref,
    wpt_ref,
    wot_ref,
    w1t_ref,
    w2t_ref,
    wp_ref,
    wo_ref,
    w1_ref,
    w2_ref,
    y_out,
    dx_out,
    half_outs,
    narrow_out,
    q_ref,
    k_ref,
    v_ref,
    p_ref,
    turned_ref,
    gate_ref,
    linv_ref,
    att_ref,
    mixed_ref,
    act_ref,
    slope_ref,
    hidden_ref,
    dmixed_ref,
    dlogit_ref,
    dproj_ref,
    dwp_ref,
    dw1_ref,
    dw2t_ref,
    dwot_ref,
    dwg_ref,
    dg1_ref,
    dg2_ref,
    xs_ref,
    cots_ref,
    ys_ref,
    dxs_ref,
    y_buf,
    dx_buf,
    y_send,
    y_recv,
    dx_send,
    dx_recv,
    local_sem,
    bias_ref,
    cos_ref,
    sin_ref,
    valid_ref,
    halves,
    core_recvs,
    core_sems,
    half_sem,
):
    step = pl.program_id(0)
    slot_count, part_frames, model = x_ref.shape
    inner, tokens = q_ref.shape
    size = inner // heads
    groups = tokens // BLOCK
    taken = tokens // slot_count
    per_part = part_frames // taken
    part = step // per_part
    first = lax.rem(step, per_part) * taken
    my_band, my_batch = lax.axis_index("band"), lax.axis_index("batch")
    slot_dev = slot_count // band_count
    slots = slot_dev // batch_count
    own_chunk = my_batch * band_count + my_band
    chunks = band_count * batch_count

    columns = [slice(at, at + 128) for at in range(0, model, 128)]

    def tokens_of(ref):
        return jnp.concatenate(
            [
                jnp.concatenate(
                    [ref[c, pl.ds(first + i, slot_count, stride=part_frames), :] for i in range(taken)], axis=0
                ).T
                for c in range(len(columns))
            ],
            axis=0,
        )

    def put_tokens(ref, values, start, stride):
        for c, at in enumerate(columns):
            turned = values[at].T
            for i in range(taken):
                ref[c, pl.ds(start + i, slot_count, stride=stride), :] = turned[
                    i * slot_count : (i + 1) * slot_count
                ]

    @pl.when(step == 0)
    def enter():
        greet_all(band_count, batch_count)
        bands = slots_ref[...].reshape(1, slot_count)
        cos, sin = rotary_rows(jnp.maximum(bands, 0).astype(F32), size // 2)
        cos_ref[...] = jnp.concatenate([cos] * taken, axis=1)
        sin_ref[...] = jnp.concatenate([sin] * taken, axis=1)
        valid = jnp.concatenate([jnp.where(bands >= 0, 1.0, 0.0)] * taken, axis=1)
        valid_ref[...] = valid
        keys = jnp.broadcast_to(valid[:, :BLOCK], (8, BLOCK)).T[:, :1]
        row = lax.broadcasted_iota(jnp.int32, (BLOCK, BLOCK), 0) // slot_count
        column_index = lax.broadcasted_iota(jnp.int32, (BLOCK, BLOCK), 1) // slot_count
        bias_ref[...] = jnp.where((row == column_index) & (keys > 0.5), 0.0, NEG_FILL)

    @pl.when(lax.rem(step, per_part) == 0)
    def unpack():
        for c, at in enumerate(columns):
            xs_ref[c] = x_ref[:, :, at].astype(F32).reshape(xs_ref.shape[1:])
            cots_ref[c] = cot_ref[:, :, at].astype(F32).reshape(cots_ref.shape[1:])

    place = Place()
    totals = [
        Total(place, order, core_sems.at[0, i], core_sems.at[1, i]) for i, order in enumerate(BAND_ORDERS)
    ]
    gain1, gain2 = column(g1_ref), column(g2_ref)
    piece = part_frames * (pl.num_programs(0) // per_part)
    own_start = (my_batch * band_count + my_band) * piece

    @pl.when(step == 0)
    def clear():
        for ref in (dwp_ref, dw1_ref, dw2t_ref, dwot_ref, dwg_ref, dg1_ref, dg2_ref):
            ref[...] = jnp.zeros_like(ref)

    rows = tokens_of(xs_ref)
    normed = norm_forward(rows, gain1)
    q_ref[...], k_ref[...], v_ref[...] = project_block(
        normed, wpt_ref, cos_ref[...], sin_ref[...], inner, LOG2E * size**-0.5
    )
    gate_ref[...] = dg(wgt_ref[...], normed, NN)
    ones = extra_rows([jnp.ones((1, BLOCK), F32)], BLOCK)
    nothing = jnp.zeros((size, BLOCK), BF16)

    def apart(first, second):
        return jnp.concatenate(
            [jnp.concatenate([first, nothing], axis=1), jnp.concatenate([nothing, second], axis=1)], axis=0
        )

    turned_ref[...] = k_ref[...].T
    bias = jnp.concatenate([bias_ref[...]] * 2, axis=1)

    def attend(pair, carry):
        both = pl.ds(pl.multiple_of(2 * pair * size, 2 * size), 2 * size)
        at = [pl.ds(pl.multiple_of((2 * pair + i) * size, size), size) for i in range(2)]
        for group in range(groups):
            lanes = slice(group * BLOCK, (group + 1) * BLOCK)
            scores = dg(turned_ref[lanes, both], apart(*(q_ref[one, lanes] for one in at)), NN) + bias
            weights = jnp.exp2(scores - jnp.max(scores, axis=0, keepdims=True)).astype(BF16)
            p_ref[pair * groups + group] = weights
            for i, one in enumerate(at):
                row = pl.ds(2 * pair + i, 1)
                own = weights[:, i * BLOCK : (i + 1) * BLOCK]
                sums = dg(jnp.concatenate([v_ref[one, lanes], ones], axis=0), own, NN)
                inverse = 1.0 / sums[size : size + 1]
                attended = sums[:size] * inverse
                linv_ref[row, lanes] = inverse
                att_ref[one, lanes] = attended
                gate = jax.nn.sigmoid(gate_ref[row, lanes])
                mixed_ref[one, lanes] = (attended * gate).astype(BF16)
        return carry

    lax.fori_loop(0, heads // 2, attend, 0, unroll=4)
    middle = rows + dg(wot_ref[...], mixed_ref[...], NN)
    normed_ffn = norm_forward(middle, gain2)

    result = feed_forward(middle, normed_ffn, w1t_ref, w2t_ref, act_ref, slope_ref)
    frame = own_start + step * taken + lax.broadcasted_iota(jnp.int32, (1, tokens), 1) // slot_count
    mask = jnp.where(frame < count_ref[0], valid_ref[...], 0.0)
    result = result * mask
    put_tokens(ys_ref, result, 0, taken)

    couples = slot_dev // 2
    for c, at in enumerate(columns):
        y_buf[step, :, :, at] = ys_ref[c].reshape(slot_count // 2, 2 * taken, 128).astype(BF16)

    def give_row(i, carry):
        other = lax.rem(my_band + i, band_count)
        send(
            y_buf.at[step, pl.ds(other * couples, couples)],
            y_out.at[:, my_band, step],
            y_send,
            y_recv,
            other,
            my_batch,
        )
        return carry

    lax.fori_loop(1, band_count, give_row, 0)
    pltpu.make_async_copy(
        y_buf.at[step, pl.ds(my_band * couples, couples)], y_out.at[:, my_band, step], local_sem.at[0]
    ).start()

    grad = tokens_of(cots_ref) * mask
    d_middle, ffn_branch, d_hidden = ffn_backward(grad, slope_ref[...], middle, gain2, w1_ref, w2_ref, dg2_ref)
    hidden_ref[...] = d_hidden
    branch = d_middle.astype(BF16)
    dmixed_ref[...] = dg(wo_ref[...], branch, NN)

    turned_ref[...] = v_ref[...].T
    def attend_back(pair, carry):
        both = pl.ds(pl.multiple_of(2 * pair * size, 2 * size), 2 * size)
        starts = [pl.multiple_of((2 * pair + i) * size, size) for i in range(2)]
        at = [pl.ds(start, size) for start in starts]
        d_atts, minuses = [], []
        for i, one in enumerate(at):
            row = pl.ds(2 * pair + i, 1)
            d_att, minus, d_logit = head_backward(
                dmixed_ref[one, :], att_ref[one, :], gate_ref[row, :], linv_ref[row, :]
            )
            dlogit_ref[row, :] = d_logit
            d_atts.append(d_att)
            minuses.append(minus)
        for group in range(groups):
            lanes = slice(group * BLOCK, (group + 1) * BLOCK)
            weights = p_ref[pair * groups + group]
            d_weights = dg(turned_ref[lanes, both], apart(*(d_att[:, lanes] for d_att in d_atts)), NN)
            minus = jnp.concatenate([minus[:, lanes] for minus in minuses], axis=1)
            d_scores = (weights.astype(F32) * (d_weights + minus)).astype(BF16)
            cos, sin = cos_ref[:, lanes], -sin_ref[:, lanes]
            for i, one in enumerate(at):
                own = slice(i * BLOCK, (i + 1) * BLOCK)
                d_queries = dg(k_ref[one, lanes], d_scores[:, own], NN) * size**-0.5
                d_keys = dg(q_ref[one, lanes], d_scores[:, own], NT) * (1.0 / LOG2E)
                d_values = dg(d_atts[i][:, lanes], weights[:, own], NT)
                dproj_ref[one, lanes] = turn(d_queries, cos, sin).astype(BF16)
                dproj_ref[pl.ds(inner + starts[i], size), lanes] = turn(d_keys, cos, sin).astype(BF16)
                dproj_ref[pl.ds(2 * inner + starts[i], size), lanes] = d_values.astype(BF16)
        return carry

    lax.fori_loop(0, heads // 2, attend_back, 0, unroll=4)
    d_logit = jnp.concatenate([dlogit_ref[...], jnp.zeros_like(dlogit_ref)], axis=0).astype(BF16)
    d_normed = dg(wp_ref[...], dproj_ref[...], NN) + dg(wgt_ref[...], dlogit_ref[...].astype(BF16), TN)
    d_rows, terms = norm_backward(rows, gain1, d_normed)
    dg1_ref[...] += jnp.sum(terms, axis=1, keepdims=True)
    put_tokens(dxs_ref, d_middle + d_rows, 0, taken)
    for c, at in enumerate(columns):
        grouped = dxs_ref[c].reshape(band_count, slots, batch_count, taken, 128)
        grouped = jnp.concatenate([grouped[:, j][:, :, None] for j in range(slots)], axis=2)
        dx_buf[step, :, :, at] = grouped.reshape(chunks, slots * taken, 128).astype(BF16)

    def give_grad(i, carry):
        other = lax.rem(my_band * batch_count + my_batch + i, chunks)
        send(
            dx_buf.at[step, other],
            dx_out.at[own_chunk, step],
            dx_send,
            dx_recv,
            other // batch_count,
            lax.rem(other, batch_count),
        )
        return carry

    lax.fori_loop(1, chunks, give_grad, 0)
    pltpu.make_async_copy(
        dx_buf.at[step, my_band * batch_count + my_batch], dx_out.at[own_chunk, step], local_sem.at[1]
    ).start()

    dwp_ref[...] += dg(normed, dproj_ref[...], NT)
    dwg_ref[...] += dg(normed, d_logit, NT)[:, :heads]
    dwot_ref[...] += dg(branch, mixed_ref[...], NT)
    add_ffn_sums(dw1_ref, dw2t_ref, ffn_branch, act_ref[...], normed_ffn, hidden_ref[...])

    @pl.when(step == pl.num_programs(0) - 1)
    def finish():
        narrow_out[...] = narrow_tile([dwg_ref[...], dg1_ref[...], dg2_ref[...]], model)
        core = place.bits["core"]
        for i, ref in enumerate((dwp_ref, dw1_ref, dw2t_ref, dwot_ref)):
            lay_halves(halves[i], 0, ref)
            totals[i].start_core(halves[i], core_recvs[i])
        for i, total in enumerate(totals):
            total.end_core(halves[i].at[core], core_recvs[i])
            pltpu.make_async_copy(halves[i].at[core], half_outs[i], half_sem.at[i]).start()
        for i in range(len(totals)):
            pltpu.make_async_copy(halves[i].at[core], half_outs[i], half_sem.at[i]).wait()
        await_bytes(y_out.at[:, 0], local_sem.at[0])
        await_bytes(dx_out.at[0], local_sem.at[1])
        for sem in (y_send, y_recv):
            await_bytes(y_out.at[:, pl.ds(0, band_count - 1)], sem)
        for sem in (dx_send, dx_recv):
            await_bytes(dx_out.at[pl.ds(0, chunks - 1)], sem)


def band_layer(rows, cot, counts, slot_bands, g1, g2, params, flips, band_count, batch_count):
    project, gating, output_weight, expand, shrink = params
    slot_count, piece, model = rows.shape
    tokens = 2 * BLOCK
    steps = slot_count * piece // tokens
    heads, inner, hidden = gating.shape[0], output_weight.shape[0], expand.shape[1]
    groups = tokens // BLOCK
    taken = tokens // slot_count
    part_frames = 16
    per_part = part_frames // taken
    slots = slot_count // (band_count * batch_count)
    slot_dev = slot_count // band_count
    consts = (slot_bands, g1, g2, gating) + flips + (project, output_weight, expand, shrink)
    widths = (3 * inner, hidden, hidden, inner)
    chunks = band_count * batch_count
    blocks = pl.BlockSpec((slot_count, part_frames, model), lambda i: (0, i // per_part, 0))
    anywhere = pl.BlockSpec(memory_space=pl.ANY)
    dma = pltpu.SemaphoreType.DMA
    return pl.pallas_call(
        lambda *refs: band_kernel(heads, batch_count, band_count, *refs),
        grid=(steps,),
        out_shape=(
            jax.ShapeDtypeStruct((slot_dev // 2, band_count, steps, 2 * taken, model), BF16),
            jax.ShapeDtypeStruct((chunks, steps, slots * taken, model), BF16),
            [jax.ShapeDtypeStruct((model // 2, width), BF16) for width in widths],
            jax.ShapeDtypeStruct((model, 128), F32),
        ),
        in_specs=[blocks, blocks, pl.BlockSpec(memory_space=pltpu.SMEM)] + [whole_spec(c) for c in consts],
        out_specs=(
            anywhere,
            anywhere,
            [anywhere for _ in widths],
            pl.BlockSpec((model, 128), lambda i: (0, 0)),
        ),
        scratch_shapes=[
            pltpu.VMEM((inner, tokens), BF16),
            pltpu.VMEM((inner, tokens), BF16),
            pltpu.VMEM((inner, tokens), BF16),
            pltpu.VMEM((heads // 2 * groups, BLOCK, 2 * BLOCK), BF16),
            pltpu.VMEM((tokens, inner), BF16),
            pltpu.VMEM((heads, tokens), F32),
            pltpu.VMEM((heads, tokens), F32),
            pltpu.VMEM((inner, tokens), F32),
            pltpu.VMEM((inner, tokens), BF16),
            pltpu.VMEM((hidden, tokens), BF16),
            pltpu.VMEM((hidden, tokens), BF16),
            pltpu.VMEM((hidden, tokens), BF16),
            pltpu.VMEM((inner, tokens), F32),
            pltpu.VMEM((heads, tokens), F32),
            pltpu.VMEM((3 * inner, tokens), BF16),
            pltpu.VMEM((model, 3 * inner), F32),
            pltpu.VMEM((model, hidden), F32),
            pltpu.VMEM((model, hidden), F32),
            pltpu.VMEM((model, inner), F32),
            pltpu.VMEM((model, heads), F32),
            pltpu.VMEM((model, 1), F32),
            pltpu.VMEM((model, 1), F32),
            pltpu.VMEM((model // 128, slot_count * part_frames, 128), F32),
            pltpu.VMEM((model // 128, slot_count * part_frames, 128), F32),
            pltpu.VMEM((model // 128, tokens, 128), F32),
            pltpu.VMEM((model // 128, tokens, 128), F32),
            pltpu.VMEM((steps, slot_count // 2, 2 * taken, model), BF16),
            pltpu.VMEM((steps, chunks, slots * taken, model), BF16),
            dma,
            dma,
            dma,
            dma,
            dma((2,)),
            pltpu.VMEM((BLOCK, BLOCK), F32),
            pltpu.VMEM((inner // heads // 2, tokens), F32),
            pltpu.VMEM((inner // heads // 2, tokens), F32),
            pltpu.VMEM((1, tokens), F32),
            [pltpu.VMEM((2, model // 2, width), BF16) for width in widths],
            [pltpu.VMEM((model // 2, width), BF16) for width in widths],
            dma((2, len(widths), TOTAL_STEPS)),
            dma((len(widths),)),
        ],
        compiler_params=pltpu.CompilerParams(
            vmem_limit_bytes=VMEM_BYTES, collective_id=1, has_side_effects=True
        ),
        cost_estimate=cost(30.0e6 * slot_count * piece, 0, 60e6),
        name="band_layer",
    )(rows, cot, counts, *consts)


def slot_shards(activations, cotangent, frame_counts, slot_bands, *weights):
    slot_dev, _, frame_dev, model = activations.shape
    batch, band = lax.axis_size("batch"), lax.axis_size("band")
    g1, wp, wg, wo, g2, w1, w2 = weights[:7]
    band_g1, band_wp, band_wg, band_wo, band_g2, band_w1, band_w2 = weights[7:]
    heads = wg.shape[1]
    time_params = (wp, wg.T, wo, w1, w2)
    band_params = (band_wp, band_wg.T, band_wo, band_w1, band_w2)
    band_rows, band_cot, rows, n, q, k, v, p, linv, gate, att, mixed, mid, nf, act, slope, *turned = time_forward(
        activations.reshape(slot_dev, frame_dev, model),
        cotangent.reshape(slot_dev, frame_dev, model),
        frame_counts,
        g1,
        g2,
        time_params,
        band_params,
        band,
        batch,
    )
    cos, sin = turned[-2:]
    y, slot_grad, band_halves, band_narrow = band_layer(
        band_rows,
        band_cot,
        frame_counts,
        slot_bands,
        band_g1,
        band_g2,
        band_params,
        tuple(turned[:-2]),
        band,
        batch,
    )
    dmid, datt, minus, dlogit, ffn_halves, dg2, band_parts = time_ffn_backward(
        slot_grad, act, slope, nf, mid, mixed, att, gate, linv, g2, w1, w2, wo, band_halves
    )
    input_grad, band_sums, ffn_sums, pair_sums = time_attention_backward(
        p,
        q,
        k,
        v,
        datt,
        minus,
        dlogit,
        n,
        rows,
        dmid,
        cos,
        sin,
        g1,
        wp,
        time_params[1],
        band_narrow,
        dg2,
        band_parts,
        ffn_halves,
        batch,
    )
    layer_output, input_grad, *grads = finish_sums(
        input_grad, y, band_sums, ffn_sums, pair_sums, g1, time_params
    )
    grads = [g.T if g.shape[0] == heads else g for g in grads]
    return (layer_output.reshape(activations.shape), input_grad.reshape(activations.shape), *grads)


def shards(activations, cotangent, frame_counts, slot_bands, *weights):
    slot_dev, clips, frame_dev, _ = activations.shape
    batch, band = lax.axis_size("batch"), lax.axis_size("band")
    fits = (
        clips == 1
        and batch == 4
        and band == 2 * Z_COUNT
        and slot_dev % batch == 0
        and frame_dev == BLOCK
        and frame_dev == 32 * band
        and slot_bands.shape[0] == 64 == slot_dev * band
        and slot_dev == 2 * batch
        and activations.shape[-1] % 128 == 0
        and (frame_dev // band * slot_bands.shape[0]) % (2 * BLOCK) == 0
        and weights[2].shape[1] == 8
    )
    form = slot_shards if fits else generic_shards
    return form(activations, cotangent, frame_counts, slot_bands, *weights)


def solution(mesh):
    return jax.shard_map(
        shards,
        mesh=mesh,
        in_specs=(
            P("band", None, "batch", None),
            P("band", None, "batch", None),
            P(),
            P(),
            P(),
            P(),
            P(),
            P(),
            P(),
            P(),
            P(),
            P(),
            P(),
            P(),
            P(),
            P(),
            P(),
            P(),
        ),
        out_specs=(
            P("band", None, "batch", None),
            P("band", None, "batch", None),
            P(),
            P(),
            P(),
            P(),
            P(),
            P(),
            P(),
            P(),
            P(),
            P(),
            P(),
            P(),
            P(),
            P(),
        ),
        check_vma=False,
    )
```

profile of v0, /device:TPU:0, one launch (start us, length us, event | category | flops | bytes accessed | tf_op | source)
XLA Modules:
  0.0 334.8 jit_solution(1404062985701421850)
XLA Ops:
  1.3 91.6 %time_forward.1 = (bf16[64,32,384]{2,1,0:T(8,128)(2,1)}, bf16[64,32,384]{2,1,0:T(8,128)(2,1)}, bf16[2,1024,384]{2,1,0:T(8,128)(2,1)}, bf16[2,384,1024]{2,1,0:T(8...) custom-call(bf16[8,256,384]{2,1,0:T(8,128)(2,1)} %bitcast.16, ...), custom_call_target="tpu_custom_call" | custom-call | flops 16384000000 | bytes 60000000 | tf_op jit(solution)/shard_map/time_forward/pallas_call | solution.py:1009
  92.9 91.7 %band_layer.1 = (bf16[4,8,4,16,384]{4,3,2,1,0:T(8,128)(2,1)}, bf16[32,4,16,384]{3,2,1,0:T(8,128)(2,1)}, bf16[192,1536]{1,0:T(8,128)(2,1)}, bf16[192,1536]{1,0:T(...) custom-call(bf16[64,32,384]{2,1,0:T(8,128)(2,1)} %get-tuple-element.86.refs_0_, ...), custom_call_target="tpu_custom_call" | custom-call | flops 61440000000 | bytes 60000000 | tf_op jit(solution)/shard_map/band_layer/pallas_call | solution.py:2125
  184.6 37.0 %time_ffn_backward.1 = (f32[2,384,1024]{2,1,0:T(8,128)}, bf16[2,512,1024]{2,1,0:T(8,128)(2,1)}, f32[2,8,1024]{2,1,0:T(8,128)}, f32[2,8,1024]{2,1,0:T(8,128)}, bf...) custom-call(bf16[32,4,16,384]{3,2,1,0:T(8,128)(2,1)} %get-tuple-elem, ...), custom_call_target="tpu_custom_call" | custom-call | flops 16384000000 | bytes 30000000 | tf_op jit(solution)/shard_map/time_ffn_backward/pallas_call | solution.py:1226
  221.6 98.8 %time_attention_backward.1 = (bf16[8,256,384]{2,1,0:T(8,128)(2,1)}, bf16[384,1536]{1,0:T(8,128)(2,1)}, bf16[384,1536]{1,0:T(8,128)(2,1)}, bf16[384,1536]{1,0:T(8...) custom-call(bf16[2,8,1024,1024]{3,2,1,0:T(8,128)(2,1)} %get-tuple-el, ...), custom_call_target="tpu_custom_call" | custom-call | flops 40960000000 | bytes 60000000 | tf_op jit(solution)/shard_map/time_attention_backward/pallas_call | solution.py:1609
  320.4 14.3 %finish_sums.1 = (bf16[8,256,384]{2,1,0:T(8,128)(2,1)}, f32[8,256,384]{2,1,0:T(8,128)}, f32[384]{0:T(512)}, f32[384,1536]{1,0:T(8,128)}, f32[8,384]{1,0:T(8,128)...) custom-call(bf16[8,256,384]{2,1,0:T(8,128)(2,1)} %get-tuple-element., ...), custom_call_target="tpu_custom_call" | custom-call | tf_op jit(solution)/shard_map/finish_sums/pallas_call | solution.py:1773
where the time goes:
time: 335 us
  Pallas kernels  333 us (99%)
    pallas_call x1, Pallas kernels, time_attention_backward(): pl.pallas_call(lambda *refs: time_attention_backward_kernel(heads, slots,...  98.8 us
    pallas_call x1, Pallas kernels, band_layer(): pl.pallas_call(lambda *refs: band_kernel(heads, batch_count, band_count,...  91.7 us
    pallas_call x1, Pallas kernels, time_forward(): pl.pallas_call(lambda *refs: time_forward_kernel(heads, batch_count, band...  91.6 us
    pallas_call x1, Pallas kernels, time_ffn_backward(): pl.pallas_call(lambda *refs: time_ffn_backward_kernel(heads, *refs), grid...  37 us
    pallas_call x1, Pallas kernels, finish_sums(): pl.pallas_call(lambda *refs: finish_kernel(heads, *refs), grid=(pairs,),...  14.3 us

commit v1 on v0

--- a/solution.py
+++ b/solution.py
@@ -548,6 +548,14 @@
     pltpu.make_async_copy(ref, ref, sem).wait()
 
 
+def by_rows(rows, action):
+    def block(i, carry):
+        action(pl.multiple_of(i * 16, 16))
+        return carry
+
+    lax.fori_loop(0, rows // 16, block, 0)
+
+
 class Place:
     def __init__(self):
         self.band, self.batch = lax.axis_index("band"), lax.axis_index("batch")
@@ -597,15 +605,19 @@
         await_bytes(ref, self.recvs.at[step])
         await_bytes(ref, self.sends.at[step])
 
-    def add(self, ref, rows, part):
-        ref[rows] = (ref[rows].astype(F32) + part.astype(F32)).astype(BF16)
+    def add(self, ref, start, part):
+        def some(i):
+            at, own = pl.ds(pl.multiple_of(start + i, 16), 16), pl.ds(i, 16)
+            ref[at] = (ref[at].astype(F32) + part[own].astype(F32)).astype(BF16)
+
+        by_rows(part.shape[0], some)
 
     def start_core(self, source, recv):
         self.give(0, source.at[1 - self.core], recv, self.place.across("core"))
 
     def end_core(self, held, recv):
         self.took(0, recv)
-        held[...] = (held[...].astype(F32) + recv[...].astype(F32)).astype(BF16)
+        self.add(held, 0, recv)
 
     def half_rows(self, held, level):
         rows = held.shape[0] // 2
@@ -623,7 +635,7 @@
 
     def end_half(self, level, held, recv):
         self.took(level, recv)
-        self.add(held, self.half_rows(held, level)[0], recv[...])
+        self.add(held, self.half_rows(held, level)[0].start, recv)
 
     def start_z(self, piece, recv):
         width = recv.shape[2]
@@ -658,22 +670,28 @@
         self.took(4, target.at[:, pl.ds(0, (Z_COUNT - 1) * width)])
         self.own_copy(piece, target, width, sem).wait()
 
-    def around(self):
-        found = []
-        for step in range(1, 4 * Z_COUNT):
-            x = lax.rem(self.place.bits["x"] + step // 2 % 2, 2)
-            y = lax.rem(self.place.bits["y"] + step % 2, 2)
-            z = lax.rem(self.place.z + step // 4, Z_COUNT)
-            found.append((2 * x + y, z, (2 * z + y, 2 * x + self.core)))
-        return found
+    def chip(self, step):
+        x = lax.rem(self.place.bits["x"] + lax.rem(step // 2, 2), 2)
+        y = lax.rem(self.place.bits["y"] + lax.rem(step, 2), 2)
+        z = lax.rem(self.place.z + step // 4, Z_COUNT)
+        return 2 * x + y, z, (2 * z + y, 2 * x + self.core)
+
+    def around(self, action):
+        def one(step, carry):
+            action(step, *self.chip(step))
+            return carry
+
+        lax.fori_loop(1, 4 * Z_COUNT, one, 0)
 
     def tile(self, ref, base, quarter, z, shape):
         rows = pl.ds(pl.multiple_of(base + quarter * shape[0], shape[0]), shape[0])
         return ref.at[rows, pl.ds(pl.multiple_of(z * shape[1], 128), shape[1])]
 
     def start_around(self, held, recv):
-        for i, (quarter, z, other) in enumerate(self.around()):
-            self.give(1, self.tile(held, 0, quarter, z, recv.shape[1:]), recv.at[i], other)
+        def one(step, quarter, z, other):
+            self.give(1, self.tile(held, 0, quarter, z, recv.shape[1:]), recv.at[step - 1], other)
+
+        self.around(one)
 
     def own_tile(self, ref, base, shape):
         return self.tile(ref, base, 2 * self.place.bits["x"] + self.place.bits["y"], self.place.z, shape)
@@ -690,8 +708,7 @@
         shape = recv.shape[1:]
         own = self.own_tile(held, 0, shape)
         target = self.own_tile(out, self.core * (out.shape[0] // 2), shape)
-        for _, _, other in self.around():
-            self.give(2, own, target, other)
+        self.around(lambda step, quarter, z, other: self.give(2, own, target, other))
         pltpu.make_async_copy(own, target, sem).start()
 
     def end_around_back(self, held, recv, out, sem):
@@ -1175,7 +1192,7 @@
     @pl.when(step == last)
     def finish():
         for sums, ref in zip(sums_refs, (dw2t_ref, dw1_ref, dwot_ref)):
-            lay_halves(sums, 0, ref)
+            lay_halves(sums, ref)
         dg2_out[...] = dg2_ref[...]
         for i, (total, halves, held, recv) in list(enumerate(work))[early:]:
             total.end_half(2, held, recv[1])
@@ -1192,17 +1209,21 @@
     return jnp.concatenate(list(parts) + [jnp.zeros((rows, 128 - used), F32)], axis=1)
 
 
-def lay_halves(target, at, ref):
-    rows, width = ref.shape
+def lay_halves(target, ref):
+    half_rows = ref.shape[0] // 2
     for half in range(2):
-        target[half, :, at : at + width] = ref[half * rows // 2 : (half + 1) * rows // 2].astype(BF16)
+
+        def some(i, half=half):
+            target[half, pl.ds(i, 16), :] = ref[pl.ds(half * half_rows + i, 16), :].astype(BF16)
+
+        by_rows(half_rows, some)
 
 
 XY, YX = ("x", "y"), ("y", "x")
 BAND_ORDERS = (YX, XY, YX, XY)
 BAND_EARLY = 2
 FFN_ORDERS = (YX, XY, YX)
-PAIR_ORDERS = (YX, YX, YX, None)
+PAIR_ORDERS = (YX, YX, None, None)
 
 
 def time_ffn_backward(grad, act, slope, nf, mid, mixed, att, gate, linv, g2, w1, w2, wo, halves_in):
@@ -1271,14 +1292,9 @@
     )(grad, act, slope, nf, mid, mixed, att, gate, linv, *consts, list(halves_in))
 
 
-BAND_PLACES = ((0, 4, 7, 11, 13), (0, 4, 7, 12, 14), (0, 4, 7, 11, 16, 18), (0, 5, 8, 12, 16, 18))
-FFN_PLACES = ((0, 1, 5, 8, 12, 15, 18, 24, 25), (0, 2, 6, 10, 13, 16, 20, 24, 25), (0, 2, 6, 9, 12, 15, 18, 22, 24))
-PAIR_PLACES = (
-    (4, 5, 8, 12, 15, 18, 22, 24, 25),
-    (8, 9, 12, 15, 17, 20, 23, 24, 25),
-    (12, 13, 15, 18, 21, 24, 25, 26, 27),
-    (16, 17, 21, 24, 25),
-)
+BAND_PLACES = ((0, 2, 5, 9, 10), (0, 3, 6, 9, 10), (0, 4, 6, 10, 13, 14), (0, 5, 7, 10, 12, 13))
+FFN_PLACES = ((0, 1, 4, 6, 8, 11, 13, 16, 18), (0, 1, 4, 7, 9, 12, 14, 18, 20), (0, 2, 5, 7, 10, 12, 14, 19, 20))
+PAIR_PLACES = ((4, 5, 10, 12, 14, 16, 18, 23, 24), (8, 9, 11, 14, 16, 18, 24, 25, 26), (12, 13, 18, 24, 25), (16, 18, 22, 24, 25))
 
 
 def time_attention_backward_kernel(
@@ -1400,8 +1416,15 @@
     def enter():
         other_x = place.across("x")[1] // 2
         diagonal = (my_band, 2 * other_x + 1 - place.bits["core"])
-        chips = [other for _, _, other in own[-1].around()]
-        greet(chips + [place.across("core"), diagonal])
+        barrier = pltpu.get_barrier_semaphore()
+
+        def call(other):
+            pl.semaphore_signal(barrier, inc=1, device_id=other, device_id_type=pl.DeviceIdType.MESH)
+
+        own[-1].around(lambda step, quarter, z, other: call(other))
+        call(place.across("core"))
+        call(diagonal)
+        pl.semaphore_wait(barrier, 4 * Z_COUNT + 1)
         for i in range(len(ffns)):
             half_copy(i).start()
 
@@ -1478,7 +1501,7 @@
         out, sem = pair_outs.at[i], local_sem.at[pair_at + i]
         recv = [ref.at[i] for ref in pair_recvs]
         if PAIR_ORDERS[i] is None:
-            actions = around_steps(own[i], source, held, [recv[0], around_recv], out, sem)
+            actions = around_steps(own[i], source, held, [recv[0], around_recv.at[PAIR_ORDERS[:i].count(None)]], out, sem)
         else:
             actions = all_steps(own[i], source, held, recv, out, sem)
         schedule(actions, PAIR_PLACES[i])
@@ -1639,7 +1662,7 @@
             [recv_buffers(width) for width in widths],
             pltpu.VMEM((pairs, 2, model // 2, pair_width), BF16),
             recv_buffers(pair_width, pairs),
-            pltpu.VMEM((4 * Z_COUNT - 1, model // 8, pair_width // Z_COUNT), BF16),
+            pltpu.VMEM((PAIR_ORDERS.count(None), 4 * Z_COUNT - 1, model // 8, pair_width // Z_COUNT), BF16),
             [dma((len(parts), TOTAL_STEPS))] * 2,
             [dma((len(widths), TOTAL_STEPS))] * 2,
             [dma((pairs, TOTAL_STEPS)), dma((pairs, TOTAL_STEPS))],
@@ -2089,7 +2112,7 @@
         narrow_out[...] = narrow_tile([dwg_ref[...], dg1_ref[...], dg2_ref[...]], model)
         core = place.bits["core"]
         for i, ref in enumerate((dwp_ref, dw1_ref, dw2t_ref, dwot_ref)):
-            lay_halves(halves[i], 0, ref)
+            lay_halves(halves[i], ref)
             totals[i].start_core(halves[i], core_recvs[i])
         for i, total in enumerate(totals):
             total.end_core(halves[i].at[core], core_recvs[i])

time: 335 us -> 327 us (0.976)
  Pallas kernels: 333 us -> 325 us
    pallas_call x1, Pallas kernels: 98.8 us -> 89.9 us  [time_attention_backward(): pl.pallas_call(lambda *refs: time_attention_backward_kernel(heads, slots,...]
where the time goes in v1:
time: 327 us; the launch traced here: 326 us
  Pallas kernels  325 us (99%)
    pallas_call x1, Pallas kernels, band_layer(): pl.pallas_call(lambda *refs: band_kernel(heads, batch_count, band_count,...  91.7 us
    pallas_call x1, Pallas kernels, time_forward(): pl.pallas_call(lambda *refs: time_forward_kernel(heads, batch_count, band...  91.6 us
    pallas_call x1, Pallas kernels, time_attention_backward(): pl.pallas_call(lambda *refs: time_attention_backward_kernel(heads, slots,...  89.9 us
    pallas_call x1, Pallas kernels, time_ffn_backward(): pl.pallas_call(lambda *refs: time_ffn_backward_kernel(heads, *refs), grid...  37.4 us
    pallas_call x1, Pallas kernels, finish_sums(): pl.pallas_call(lambda *refs: finish_kernel(heads, *refs), grid=(pairs,),...  14.3 us

profile of v1, /device:TPU:0, one launch (start us, length us, event | category | flops | bytes accessed | tf_op | source)
XLA Modules:
  0.0 326.4 jit_solution(9318649525831746826)
XLA Ops:
  1.3 91.6 %time_forward.1 = (bf16[64,32,384]{2,1,0:T(8,128)(2,1)}, bf16[64,32,384]{2,1,0:T(8,128)(2,1)}, bf16[2,1024,384]{2,1,0:T(8,128)(2,1)}, bf16[2,384,1024]{2,1,0:T(8...) custom-call(bf16[8,256,384]{2,1,0:T(8,128)(2,1)} %bitcast.16, ...), custom_call_target="tpu_custom_call" | custom-call | flops 16384000000 | bytes 60000000 | tf_op jit(solution)/shard_map/time_forward/pallas_call | solution.py:1026
  92.9 91.7 %band_layer.1 = (bf16[4,8,4,16,384]{4,3,2,1,0:T(8,128)(2,1)}, bf16[32,4,16,384]{3,2,1,0:T(8,128)(2,1)}, bf16[192,1536]{1,0:T(8,128)(2,1)}, bf16[192,1536]{1,0:T(...) custom-call(bf16[64,32,384]{2,1,0:T(8,128)(2,1)} %get-tuple-element.86.refs_0_, ...), custom_call_target="tpu_custom_call" | custom-call | flops 61440000000 | bytes 60000000 | tf_op jit(solution)/shard_map/band_layer/pallas_call | solution.py:2148
  184.6 37.4 %time_ffn_backward.1 = (f32[2,384,1024]{2,1,0:T(8,128)}, bf16[2,512,1024]{2,1,0:T(8,128)(2,1)}, f32[2,8,1024]{2,1,0:T(8,128)}, f32[2,8,1024]{2,1,0:T(8,128)}, bf...) custom-call(bf16[32,4,16,384]{3,2,1,0:T(8,128)(2,1)} %get-tuple-elem, ...), custom_call_target="tpu_custom_call" | custom-call | flops 16384000000 | bytes 30000000 | tf_op jit(solution)/shard_map/time_ffn_backward/pallas_call | solution.py:1247
  222.0 89.9 %time_attention_backward.1 = (bf16[8,256,384]{2,1,0:T(8,128)(2,1)}, bf16[384,1536]{1,0:T(8,128)(2,1)}, bf16[384,1536]{1,0:T(8,128)(2,1)}, bf16[384,1536]{1,0:T(8...) custom-call(bf16[2,8,1024,1024]{3,2,1,0:T(8,128)(2,1)} %get-tuple-el, ...), custom_call_target="tpu_custom_call" | custom-call | flops 40960000000 | bytes 60000000 | tf_op jit(solution)/shard_map/time_attention_backward/pallas_call | solution.py:1632
  311.9 14.3 %finish_sums.1 = (bf16[8,256,384]{2,1,0:T(8,128)(2,1)}, f32[8,256,384]{2,1,0:T(8,128)}, f32[384]{0:T(512)}, f32[384,1536]{1,0:T(8,128)}, f32[8,384]{1,0:T(8,128)...) custom-call(bf16[8,256,384]{2,1,0:T(8,128)(2,1)} %get-tuple-element., ...), custom_call_target="tpu_custom_call" | custom-call | tf_op jit(solution)/shard_map/finish_sums/pallas_call | solution.py:1796

commit v2 on v1

--- a/solution.py
+++ b/solution.py
@@ -1952,9 +1952,10 @@
 
     @pl.when(lax.rem(step, per_part) == 0)
     def unpack():
+        held = slot_count * part_frames
         for c, at in enumerate(columns):
-            xs_ref[c] = x_ref[:, :, at].astype(F32).reshape(xs_ref.shape[1:])
-            cots_ref[c] = cot_ref[:, :, at].astype(F32).reshape(cots_ref.shape[1:])
+            xs_ref[c, pl.ds(0, held)] = x_ref[:, :, at].astype(F32).reshape(held, 128)
+            cots_ref[c, pl.ds(0, held)] = cot_ref[:, :, at].astype(F32).reshape(held, 128)
 
     place = Place()
     totals = [
@@ -2018,7 +2019,7 @@
 
     couples = slot_dev // 2
     for c, at in enumerate(columns):
-        y_buf[step, :, :, at] = ys_ref[c].reshape(slot_count // 2, 2 * taken, 128).astype(BF16)
+        y_buf[step, :, :, at] = ys_ref[c, pl.ds(0, tokens)].reshape(slot_count // 2, 2 * taken, 128).astype(BF16)
 
     def give_row(i, carry):
         other = lax.rem(my_band + i, band_count)
@@ -2081,7 +2082,7 @@
     dg1_ref[...] += jnp.sum(terms, axis=1, keepdims=True)
     put_tokens(dxs_ref, d_middle + d_rows, 0, taken)
     for c, at in enumerate(columns):
-        grouped = dxs_ref[c].reshape(band_count, slots, batch_count, taken, 128)
+        grouped = dxs_ref[c, pl.ds(0, tokens)].reshape(band_count, slots, batch_count, taken, 128)
         grouped = jnp.concatenate([grouped[:, j][:, :, None] for j in range(slots)], axis=2)
         dx_buf[step, :, :, at] = grouped.reshape(chunks, slots * taken, 128).astype(BF16)
 
@@ -2184,10 +2185,10 @@
             pltpu.VMEM((model, heads), F32),
             pltpu.VMEM((model, 1), F32),
             pltpu.VMEM((model, 1), F32),
-            pltpu.VMEM((model // 128, slot_count * part_frames, 128), F32),
-            pltpu.VMEM((model // 128, slot_count * part_frames, 128), F32),
-            pltpu.VMEM((model // 128, tokens, 128), F32),
-            pltpu.VMEM((model // 128, tokens, 128), F32),
+            pltpu.VMEM((model // 128, (slot_count + 1) * part_frames, 128), F32),
+            pltpu.VMEM((model // 128, (slot_count + 1) * part_frames, 128), F32),
+            pltpu.VMEM((model // 128, tokens + taken, 128), F32),
+            pltpu.VMEM((model // 128, tokens + taken, 128), F32),
             pltpu.VMEM((steps, slot_count // 2, 2 * taken, model), BF16),
             pltpu.VMEM((steps, chunks, slots * taken, model), BF16),
             dma,

time: 327 us -> 327 us (level)
  no operation moved by 1% of the time
where the time goes in v2:
time: 327 us; the launch traced here: 326 us
  Pallas kernels  325 us (99%)
    pallas_call x1, Pallas kernels, band_layer(): pl.pallas_call(lambda *refs: band_kernel(heads, batch_count, band_count,...  91.7 us
    pallas_call x1, Pallas kernels, time_forward(): pl.pallas_call(lambda *refs: time_forward_kernel(heads, batch_count, band...  91.6 us
    pallas_call x1, Pallas kernels, time_attention_backward(): pl.pallas_call(lambda *refs: time_attention_backward_kernel(heads, slots,...  89.9 us
    pallas_call x1, Pallas kernels, time_ffn_backward(): pl.pallas_call(lambda *refs: time_ffn_backward_kernel(heads, *refs), grid...  37.4 us
    pallas_call x1, Pallas kernels, finish_sums(): pl.pallas_call(lambda *refs: finish_kernel(heads, *refs), grid=(pairs,),...  14.3 us

profile of v2, /device:TPU:0, one launch (start us, length us, event | category | flops | bytes accessed | tf_op | source)
XLA Modules:
  0.0 326.4 jit_solution(9209364143050682887)
XLA Ops:
  1.3 91.6 %time_forward.1 = (bf16[64,32,384]{2,1,0:T(8,128)(2,1)}, bf16[64,32,384]{2,1,0:T(8,128)(2,1)}, bf16[2,1024,384]{2,1,0:T(8,128)(2,1)}, bf16[2,384,1024]{2,1,0:T(8...) custom-call(bf16[8,256,384]{2,1,0:T(8,128)(2,1)} %bitcast.16, ...), custom_call_target="tpu_custom_call" | custom-call | flops 16384000000 | bytes 60000000 | tf_op jit(solution)/shard_map/time_forward/pallas_call | solution.py:1026
  92.9 91.7 %band_layer.1 = (bf16[4,8,4,16,384]{4,3,2,1,0:T(8,128)(2,1)}, bf16[32,4,16,384]{3,2,1,0:T(8,128)(2,1)}, bf16[192,1536]{1,0:T(8,128)(2,1)}, bf16[192,1536]{1,0:T(...) custom-call(bf16[64,32,384]{2,1,0:T(8,128)(2,1)} %get-tuple-element.86.refs_0_, ...), custom_call_target="tpu_custom_call" | custom-call | flops 61440000000 | bytes 60000000 | tf_op jit(solution)/shard_map/band_layer/pallas_call | solution.py:2149
  184.6 37.4 %time_ffn_backward.1 = (f32[2,384,1024]{2,1,0:T(8,128)}, bf16[2,512,1024]{2,1,0:T(8,128)(2,1)}, f32[2,8,1024]{2,1,0:T(8,128)}, f32[2,8,1024]{2,1,0:T(8,128)}, bf...) custom-call(bf16[32,4,16,384]{3,2,1,0:T(8,128)(2,1)} %get-tuple-elem, ...), custom_call_target="tpu_custom_call" | custom-call | flops 16384000000 | bytes 30000000 | tf_op jit(solution)/shard_map/time_ffn_backward/pallas_call | solution.py:1247
  222.0 89.9 %time_attention_backward.1 = (bf16[8,256,384]{2,1,0:T(8,128)(2,1)}, bf16[384,1536]{1,0:T(8,128)(2,1)}, bf16[384,1536]{1,0:T(8,128)(2,1)}, bf16[384,1536]{1,0:T(8...) custom-call(bf16[2,8,1024,1024]{3,2,1,0:T(8,128)(2,1)} %get-tuple-el, ...), custom_call_target="tpu_custom_call" | custom-call | flops 40960000000 | bytes 60000000 | tf_op jit(solution)/shard_map/time_attention_backward/pallas_call | solution.py:1632
  311.9 14.3 %finish_sums.1 = (bf16[8,256,384]{2,1,0:T(8,128)(2,1)}, f32[8,256,384]{2,1,0:T(8,128)}, f32[384]{0:T(512)}, f32[384,1536]{1,0:T(8,128)}, f32[8,384]{1,0:T(8,128)...) custom-call(bf16[8,256,384]{2,1,0:T(8,128)(2,1)} %get-tuple-element., ...), custom_call_target="tpu_custom_call" | custom-call | tf_op jit(solution)/shard_map/finish_sums/pallas_call | solution.py:1796
